TPU v7x, 256 devices: a whole 4x4x8 slice. The times are simulated.
256 devices in a mesh: prow: 16 (over y, z_hi), pcol: 16 (over x, z_lo, core).
Axes of the slice: x: 4, y: 4, z: 8 (z_hi: 4, z_lo: 2; z = z_hi * 2 + z_lo), core: 2. Of those that a mesh axis runs over, the one named last changes fastest.
Arguments:
- covariance: float32 [96, 16, 64, 4096], P(None, 'prow', None, 'pcol'), may hold values from -32 to 6208, as said below
Outputs:
- factored: float32 [96, 16, 64, 4096], P(None, 'prow', None, 'pcol')
Inputs may be any that keep to these rules, and one draw needn't show every extreme that they name: `covariance`: in the leading 2 * 64 columns every diagonal entry exceeds 2 * 64 times the largest magnitude of the other entries of those columns, so the leading block of order 2 * 64 is positive definite.
All inputs are finite; a program needn't handle non-finite values.
Results may differ from a plain program's by a relative error of at most 0.0003.
Values sent between devices are 32-bit elements; how exact they have to be, the bound alone decides.
No kernel may reach another device: no remote copies, remote signals or barrier semaphores. Data moves between devices by JAX's collectives and lax.ppermute only.
A program may use at most 128 MiB of HBM per device.

v0:
```python
import jax
import jax.numpy as jnp
from jax import lax
from jax.sharding import PartitionSpec as P


def broadcast(value, axis, source):
    kept = jnp.where(lax.axis_index(axis) == source, value, 0).astype(value.dtype)
    return lax.psum(kept, axis)


def factor_panel(state, section, block_width, row_blocks, blocks_glob, prow_count):
    start_col = section * block_width
    slot = section // prow_count
    corner = state[
        slot * block_width : (slot + 1) * block_width, start_col : start_col + block_width
    ]
    corner = broadcast(corner, "prow", section % prow_count)
    symmetric = jnp.tril(corner) + jnp.tril(corner, -1).T
    factor_low = jnp.linalg.cholesky(symmetric)
    inverse = jax.scipy.linalg.solve_triangular(
        factor_low, jnp.eye(block_width, dtype=jnp.float32), lower=True
    )
    panel_t = jnp.dot(
        inverse, state[:, start_col : start_col + block_width].T, precision=lax.Precision.HIGHEST
    )
    shaped = panel_t.reshape(block_width, row_blocks, block_width)
    is_diagonal = blocks_glob == section
    shaped = jnp.where(is_diagonal[None, :, None], factor_low.T[:, None, :], shaped)
    return shaped.reshape(block_width, row_blocks * block_width)


def transposed_rows(rows_t, block_width, local_cols, pcol_id, prow_count, pcol_count):
    width = rows_t.shape[0]
    window_blocks = pcol_count * local_cols // block_width // prow_count
    piece = rows_t[:, : window_blocks * block_width].reshape(width, window_blocks, 1, block_width)
    gathered = lax.all_gather(piece, "prow", axis=2, tiled=True)
    gathered = gathered.reshape(width, window_blocks * prow_count * block_width)
    return lax.dynamic_slice_in_dim(gathered, pcol_id * local_cols, local_cols, 1)


def trailing_product(rows_t, cols_t):
    return lax.dot_general(
        rows_t,
        cols_t,
        (((0,), (0,)), ((), ())),
        precision=lax.Precision.HIGHEST,
        preferred_element_type=jnp.float32,
    )


def body(covariance):
    prow_count = lax.axis_size("prow")
    pcol_count = lax.axis_size("pcol")
    prow_id = lax.axis_index("prow")
    pcol_id = lax.axis_index("pcol")
    row_blocks, single, block_width, local_cols = covariance.shape
    local = covariance.reshape(row_blocks * block_width, local_cols)
    blocks_glob = jnp.arange(row_blocks, dtype=jnp.int32) * prow_count + prow_id
    rows_glob = (
        blocks_glob[:, None] * block_width + jnp.arange(block_width, dtype=jnp.int32)[None, :]
    ).reshape(-1)
    cols_glob = pcol_id * local_cols + jnp.arange(local_cols, dtype=jnp.int32)
    lower = rows_glob[:, None] >= cols_glob[None, :]
    on_first = pcol_id == 0
    state = local
    for section in range(2):
        start_col = section * block_width
        stop_col = start_col + block_width
        panel_t = factor_panel(state, section, block_width, row_blocks, blocks_glob, prow_count)
        rows_t = broadcast(panel_t, "pcol", 0)
        cols_t = transposed_rows(rows_t, block_width, local_cols, pcol_id, prow_count, pcol_count)
        product = trailing_product(rows_t, cols_t)
        update_mask = lower & (cols_glob >= stop_col)[None, :]
        changed = jnp.where(update_mask, state - product, state)
        panel_mask = lower[:, start_col:stop_col] & on_first
        panel_cols = jnp.where(panel_mask, rows_t.T, changed[:, start_col:stop_col])
        state = changed.at[:, start_col:stop_col].set(panel_cols)
    return state.reshape(row_blocks, single, block_width, local_cols)


def solution(mesh):
    placed = (P(None, "prow", None, "pcol"),)
    return jax.shard_map(
        body, mesh=mesh, in_specs=placed, out_specs=P(None, "prow", None, "pcol"), check_vma=False
    )
```

profile of v0, /device:TPU:1, one launch (start us, length us, event | category | flops | bytes accessed | tf_op | source)
XLA Modules:
  0.0 676.2 jit_solution(15163550134703504348)
XLA Ops:
  6.6 0.8 slice_select_fusion.1
  7.3 72.3 %psum.28 = f32[64,64]{1,0:T(8,128)S(1)} all-reduce(f32[64,64]{1,0:T(8,128)S(1)} %slice_select_fusion.1), channel_id=1, replica_groups=mesh['prow'=16,'pcol'=16] {'prow'}, use_global_device_ids=true, to_apply=%region_0.1 | all-reduce | flops 4096 | bytes 32768 | tf_op jit(solution)/shard_map/psum | solution.py:9
  79.6 0.1 copy.24
  79.7 0.1 bitcast_add_fusion.3
  79.8 0.1 copy.26
  79.9 5.8 cholesky.44
  85.7 0.6 compare_reduce_fusion.1
  86.4 0.7 select_bitcast_fusion.1
  87.1 4.9 custom-call.6
  92.0 0.3 fusion.8
  92.2 0.1 broadcast_in_dim.64
  92.3 0.1 broadcast_in_dim.65
  92.4 0.4 broadcast_in_dim.68
  92.8 5.5 fusion.1
  98.3 0.0 all-reduce.3.cloned.1.call-update
  98.3 0.0 all-gather.3.cloned.1.call-start
  98.4 141.8 %all-reduce.3.cloned.1.call-done = f32[64,6144]{0,1:T(8,128)} async-done(((f32[64,6144]{0,1:T(8,128)}), f32[64,6144]{0,1:T(8,128)}) %all-reduce.3.cloned.1.call-update) | async-done | bytes 1572880 | tf_op jit(solution)/shard_map/psum | solution.py:9
  240.2 0.9 slice.84
  241.1 0.8 copy.28
  241.9 0.0 all-gather.3.cloned.1.call-update
  241.9 0.0 all-reduce.5.cloned.1.call-start
  241.9 0.1 iota_add_fusion
  242.0 0.1 add.102
  242.1 0.1 copy.31
  242.2 0.1 broadcast_in_dim.71
  242.3 0.1 broadcast_in_dim.72
  242.4 0.7 compare_reduce_fusion.3
  243.1 3.6 broadcast_compare_fusion
  246.7 55.9 %all-gather.3.cloned.1.call-done = f32[64,4,16,64]{3,0,1,2:T(8,128)} async-done(((f32[64,4,1,64]{3,0,1,2:T(8,128)}), f32[64,4,16,64]{3,0,1,2:T(8,128)}) %all-gather.3.cloned.1.call-update) | async-done | bytes 1048592 | tf_op jit(solution)/shard_map/all_gather | solution.py:37
  302.5 4.1 copy.29
  306.7 2.9 reshape.127
  309.6 0.0 copy-done.2
  309.6 8.1 %subtract_select_fusion.1 = f32[6144,256]{1,0:T(8,128)S(1)} fusion(f32[6144,256]{1,0:T(8,128)} %bitcast.48, f32[64,6144]{0,1:T(8,128)S(1)} %copy-done.2, s32[256]{0:T(256)S(1)} %iota_add_fusion.1, s32[6144]{0:T(1024)S(1)} %add.102, pred[256]{0:T(512)(128)(4,1)S(1)} %fusion.16, f32[64,4096]{1,0:T(8,128)} %reshape.127, s32[]{:T(128)S(6)} %select_n.77), kind=kOutput, calls=%fused_computation.1 | convolution fusion | flops 1214251008 | bytes 14247172 | tf_op jit(solution)/shard_map/dot_general | solution.py:43
  317.7 0.0 copy-start
  317.7 2.7 copy-done
  320.4 2.9 select_select_fusion.1
  323.3 16.1 %scatter.6 = f32[6144,256]{1,0:T(8,128)} dynamic-update-slice(f32[6144,256]{1,0:T(8,128)} %copy-done, f32[6144,64]{1,0:T(8,128)} %select_select_fusion.1, s32[]{:T(128)} %constant.114.clone.1, s32[]{:T(128)} %constant.114.clone.1) | dynamic-update-slice | bytes 3145732 | tf_op jit(solution)/shard_map/scatter | solution.py:78
  339.4 0.8 slice_select_fusion
  340.2 66.1 %psum.30 = f32[64,64]{1,0:T(8,128)S(1)} all-reduce(f32[64,64]{1,0:T(8,128)S(1)} %slice_select_fusion), channel_id=1, replica_groups=mesh['prow'=16,'pcol'=16] {'prow'}, use_global_device_ids=true, to_apply=%region_5.8 | all-reduce | flops 4096 | bytes 32768 | tf_op jit(solution)/shard_map/psum | solution.py:9
  406.4 0.1 copy.32
  406.5 0.1 bitcast_add_fusion.1
  406.5 0.1 copy.33
  406.6 5.8 cholesky.55
  412.5 0.7 compare_reduce_fusion
  413.2 0.7 select_bitcast_fusion
  414.0 4.9 custom-call.7
  418.8 0.3 fusion.6
  419.1 0.4 broadcast_in_dim.74
  419.5 5.7 fusion
  425.2 0.0 all-reduce.5.cloned.1.call-update
  425.2 0.0 all-gather.5.cloned.1.call-start
  425.2 141.8 %all-reduce.5.cloned.1.call-done = f32[64,6144]{0,1:T(8,128)} async-done(((f32[64,6144]{0,1:T(8,128)}), f32[64,6144]{0,1:T(8,128)}) %all-reduce.5.cloned.1.call-update) | async-done | bytes 1572880 | tf_op jit(solution)/shard_map/psum | solution.py:9
  567.0 0.9 slice.89
  567.9 0.7 copy.35
  568.7 0.0 all-gather.5.cloned.1.call-update
  568.7 0.7 compare_reduce_fusion.2
  569.4 59.8 %all-gather.5.cloned.1.call-done = f32[64,4,16,64]{3,0,1,2:T(8,128)} async-done(((f32[64,4,1,64]{3,0,1,2:T(8,128)}), f32[64,4,16,64]{3,0,1,2:T(8,128)}) %all-gather.5.cloned.1.call-update) | async-done | bytes 1048592 | tf_op jit(solution)/shard_map/all_gather | solution.py:37
  629.2 4.2 copy.36
  633.4 2.9 reshape.129
  636.3 8.1 %subtract_select_fusion = f32[6144,256]{1,0:T(8,128)S(1)} fusion(f32[6144,256]{1,0:T(8,128)} %scatter.6, f32[64,6144]{0,1:T(8,128)S(1)} %copy-done.3, s32[256]{0:T(256)S(1)} %iota_add_fusion.1, s32[6144]{0:T(1024)S(1)} %add.102, pred[256]{0:T(512)(128)(4,1)S(1)} %fusion.17, f32[64,4096]{1,0:T(8,128)} %reshape.129, s32[]{:T(128)S(6)} %select_n.77), kind=kOutput, calls=%fused_computation | convolution fusion | flops 1214251008 | bytes 14247172 | tf_op jit(solution)/shard_map/dot_general | solution.py:43
  644.4 0.0 copy-start.1
  644.4 2.7 copy-done.1
  647.1 4.1 select_select_fusion
  651.2 18.4 %scatter.9 = f32[6144,256]{1,0:T(8,128)} dynamic-update-slice(f32[6144,256]{1,0:T(8,128)} %copy-done.1, f32[6144,64]{1,0:T(8,128)} %select_select_fusion, s32[]{:T(128)} %constant.114.clone.1, s32[]{:T(128)} %constant.111.clone.1) | dynamic-update-slice | bytes 3145732 | tf_op jit(solution)/shard_map/scatter | solution.py:78
  (21 shorter events, 0.2 us)
Async XLA Ops:
  6.5 233.7 %all-reduce.3.cloned.1.call-start = ((), (), s32[]{:S(2)}) async-start(), calls=%async_computation | async-start | bytes 6291456 | tf_op jit(solution)/shard_map/psum | solution.py:9
  98.3 204.2 %all-gather.3.cloned.1.call-start = ((), (), s32[]{:S(2)}) async-start(), calls=%async_computation.1 | async-start | bytes 2228224 | tf_op jit(solution)/shard_map/all_gather | solution.py:37
  241.9 325.1 %all-reduce.5.cloned.1.call-start = ((), (), s32[]{:S(2)}) async-start(), calls=%async_computation.2 | async-start | bytes 6291456 | tf_op jit(solution)/shard_map/psum | solution.py:9
  246.7 62.9 %copy-start.2 = (f32[64,6144]{0,1:T(8,128)S(1)}, f32[64,6144]{0,1:T(8,128)}, u32[]{:S(2)}) copy-start(f32[64,6144]{0,1:T(8,128)} %all-reduce.3.cloned.1.call-done) | copy-start | bytes 4718596
  309.6 10.8 %copy-start.4 = (pred[6144,256]{1,0:T(8,128)(4,1)S(1)}, pred[6144,256]{1,0:T(8,128)(4,1)}, u32[]{:S(2)}) copy-start(pred[6144,256]{1,0:T(8,128)(4,1)} %broadcast_compare_fusion) | copy-start | bytes 4718596
  317.7 2.7 copy-start
  425.2 204.0 %all-gather.5.cloned.1.call-start = ((), (), s32[]{:S(2)}) async-start(), calls=%async_computation.3 | async-start | bytes 2228224 | tf_op jit(solution)/shard_map/all_gather | solution.py:37
  569.4 66.9 %copy-start.3 = (f32[64,6144]{0,1:T(8,128)S(1)}, f32[64,6144]{0,1:T(8,128)}, u32[]{:S(2)}) copy-start(f32[64,6144]{0,1:T(8,128)} %all-reduce.5.cloned.1.call-done) | copy-start | bytes 4718596
  636.3 10.8 %copy-start.5 = (pred[6144,256]{1,0:T(8,128)(4,1)S(1)}, pred[6144,256]{1,0:T(8,128)(4,1)}, u32[]{:S(2)}) copy-start(pred[6144,256]{1,0:T(8,128)(4,1)} %broadcast_compare_fusion) | copy-start | bytes 4718596
  644.4 2.7 copy-start.1
Sparse Core Ops, SparseCore 0:
  98.4 141.7 all-reduce.2
  242.6 59.8 all-gather.2
  425.3 141.6 all-reduce.4
  569.3 59.8 all-gather.4
where the time goes:
time: 678 us; the launch traced here: 676 us
  waiting for transfers between devices  399 us (59%)
  blocking collectives  138 us (20%)
  local copies, waits for them, and re-layouts  59 us (9%)
  other arithmetic  38.1 us (6%)
  matrix products  27.9 us (4%)
  between operations  13.3 us (2%)
    psum x2, waiting for transfers between devices, broadcast(): return lax.psum(kept, axis)  284 us
    psum x2, blocking collectives, broadcast(): return lax.psum(kept, axis)  138 us
    all_gather x2, waiting for transfers between devices, transposed_rows(): gathered = lax.all_gather(piece, 'prow', axis=2, tiled=True)  116 us
    scatter x2, local copies, waits for them, and re-layouts, body(): state = changed.at[:, start_col:stop_col].set(panel_cols)  34.6 us
    dot_general x2, matrix products, trailing_product(): lax.dot_general(rows_t, cols_t, (((0,), (0,)), ((), ())), precision=lax.P...  16.2 us
  transfers between devices with their start and end apart: 4, of which 4 were waited for; matrix products, arithmetic and copies ran while one was open for 1% of the time, Pallas kernels for 0%

commit v1 on v0

v1 whole, which is shorter than its diff:
```python
import functools

import jax
import jax.numpy as jnp
from jax import lax
from jax.experimental import pallas as pl
from jax.experimental.pallas import tpu as pltpu
from jax.sharding import PartitionSpec as P

AXES = ("prow", "pcol")
NP, NQ = 16, 16
NB = 64
W2 = 2 * NB
PIECES = 8
F32 = jnp.float32
HI = lax.Precision.HIGHEST


def chip_move(chip, dx, dz):
    x, z = chip // 2, chip % 2
    return ((x + dx) % 4) * 2 + (z + dz) % 2


def over_pcol(value, pairs):
    flat = [(p * NQ + s, p * NQ + d) for p in range(NP) for s, d in pairs]
    return lax.ppermute(value, AXES, flat)


def over_prow(value, pairs):
    flat = [(s * NQ + q, d * NQ + q) for q in range(NQ) for s, d in pairs]
    return lax.ppermute(value, AXES, flat)


def factor_kernel(q_ref, corner_ref, lead_ref, m_ref, l_ref):
    raw = corner_ref[...]
    r = lax.broadcasted_iota(jnp.int32, (W2, W2), 0)
    c = lax.broadcasted_iota(jnp.int32, (W2, W2), 1)
    sym = jnp.where(r >= c, raw, jnp.where(r >= c, raw, 0.0).T)
    eye = jnp.where(r == c, 1.0, 0.0).astype(F32)
    full = jnp.concatenate([sym, eye], axis=1)
    tiles = [full[8 * t : 8 * t + 8] for t in range(W2 // 8)]
    sub = lax.broadcasted_iota(jnp.int32, (8, 1), 0)
    done = []
    for j in range(W2):
        t0, s0 = divmod(j, 8)
        row = tiles[t0][s0 : s0 + 1]
        row = row * lax.rsqrt(row[:, j : j + 1])
        done.append(row)
        inv = lax.rsqrt(tiles[t0][s0 : s0 + 1, j : j + 1])
        for t in range(t0, W2 // 8):
            col = tiles[t][:, j : j + 1] * inv
            if t == t0:
                col = jnp.where(sub > s0, col, 0.0)
            tiles[t] = tiles[t] - col * row
    rows = jnp.concatenate(done, axis=0)
    upper = jnp.where(r <= c, rows[:, :W2], 0.0)
    linv = jnp.where(r >= c, rows[:, W2:], 0.0)
    l_ref[...] = upper.T
    y = lax.dot_general(
        linv, lead_ref[...], (((1,), (1,)), ((), ())), precision=HI, preferred_element_type=F32
    )
    on_first = q_ref[0] == 0
    y = jnp.concatenate([jnp.where(on_first, -eye, y[:, :W2]), y[:, W2:]], axis=1)
    m_ref[...] = lax.dot_general(
        linv, y, (((0,), (0,)), ((), ())), precision=HI, preferred_element_type=F32
    )


def update_kernel(info, m_ref, l_ref, *refs):
    bufs, s_ref, o_ref, mhh, mlo = refs[:9], refs[9], refs[10], refs[11], refs[12]
    i = pl.program_id(0)
    block, core, p, q = info[i], info[8], info[9], info[10]

    @pl.when(i == 0)
    def _():
        m = m_ref[...]
        hi = m.astype(jnp.bfloat16)
        mhh[0:W2] = hi
        mhh[W2 : 2 * W2] = hi
        mlo[...] = (m - hi.astype(F32)).astype(jnp.bfloat16)

    rows, cols = s_ref.shape

    def run(buf):
        x = buf[...]
        hi = x.astype(jnp.bfloat16)
        lo = (x - hi.astype(F32)).astype(jnp.bfloat16)
        prod = jnp.dot(jnp.concatenate([hi, lo], axis=1), mhh[...], preferred_element_type=F32)
        prod += jnp.dot(hi, mlo[...], preferred_element_type=F32)
        old = s_ref[...]
        lane = lax.broadcasted_iota(jnp.int32, (1, cols), 1)
        replaced = (q == 0) & (lane < W2)
        o_ref[...] = jnp.where(replaced, 0.0, old) - prod

    for k in range(9):
        if k == 0:
            pick = i == 0
        elif k <= 2:
            pick = (i == 1) & (core == k - 1)
        else:
            pick = i == k - 1
        pl.when(pick)(functools.partial(run, bufs[k]))

    @pl.when(block == 0)
    def _():
        top = 4 * NB
        rr = lax.broadcasted_iota(jnp.int32, (top, cols), 0)
        cc = lax.broadcasted_iota(jnp.int32, (top, cols), 1) + q * cols
        rg = ((rr // NB) * NP + p) * NB + rr % NB
        o_ref[0:top] = jnp.where(rg >= cc, o_ref[0:top], s_ref[0:top])

    @pl.when((block == 0) & (q == 0) & (p < 2))
    def _():
        rr = lax.broadcasted_iota(jnp.int32, (NB, W2), 0) + p * NB
        cc = lax.broadcasted_iota(jnp.int32, (NB, W2), 1)
        part = l_ref[pl.ds(pl.multiple_of(p * NB, NB), NB), :]
        o_ref[0:NB, 0:W2] = jnp.where(rr >= cc, part, s_ref[0:NB, 0:W2])


def body(covariance):
    row_blocks, single, nb, cols = covariance.shape
    rows = row_blocks * nb
    local = covariance.reshape(rows, cols)
    p = lax.axis_index("prow")
    q = lax.axis_index("pcol")
    y, z = p // 4, p % 4
    chip, core = q // 2, q % 2
    part = rows // PIECES
    is_src = q == 0

    top = jnp.where(is_src, local[: 4 * NB, :W2], 0.0)
    have = [0]
    for bit in (1, 2, 4, 8):
        top = top + over_pcol(top, [(s, s + bit) for s in have])
        have = have + [s + bit for s in have]

    mine = jnp.where(is_src, local[:part, :W2], 0.0)
    for g in range(1, PIECES):
        mine = mine + over_pcol(local[g * part : (g + 1) * part, :W2], [(0, 2 * g)])
    both = mine + over_pcol(mine, [(2 * g, 2 * g + 1) for g in range(PIECES)])
    swap = [(s, s ^ 1) for s in range(NQ)]
    far = over_pcol(mine, [(2 * g, 2 * chip_move(g, 2, 1)) for g in range(PIECES)])
    far_s = over_pcol(far, swap)
    moves = [((1, 0), (-1, 0)), ((0, 1), (2, 0)), ((1, 1), (-1, 1))]
    bufs = [both, far, far_s]
    owners = [chip, (chip // 2 + 2) % 4 * 2 + 1 - chip % 2]
    for m0, m1 in moves:
        pairs = [(2 * g, 2 * chip_move(g, *m0)) for g in range(PIECES)]
        pairs += [(2 * g + 1, 2 * chip_move(g, *m1) + 1) for g in range(PIECES)]
        got = over_pcol(both, pairs)
        bufs += [got, over_pcol(got, swap)]
        own = [((chip // 2 - m[0]) % 4) * 2 + (chip + m[1]) % 2 for m in (m0, m1)]
        owners += [jnp.where(core == 0, own[0], own[1]), jnp.where(core == 0, own[1], own[0])]

    root = q % 4
    lead = lax.dynamic_slice_in_dim(top, (q // 4) * NB, NB, 0)
    pack = jnp.stack([lead, top[:NB]])
    got = over_prow(pack, [(s, s ^ 4) for s in range(NP)])
    use = jnp.stack([y == root ^ 1, y == 1])
    pack = jnp.where(use[:, None, None], got, pack)
    got = over_prow(pack, [(s, s ^ 8) for s in range(NP)])
    use = jnp.stack([y // 2 != root // 2, y >= 2])
    pack = jnp.where(use[:, None, None], got, pack)
    got = over_prow(pack, [(s, s ^ 1) for s in range(NP)])
    odd = z % 2 == 1
    pack = jnp.where(odd, jnp.stack([got, pack]), jnp.stack([pack, got]))
    got = over_prow(pack, [(s, s ^ 2) for s in range(NP)])
    high = z >= 2
    lead = jnp.where(
        high, jnp.stack([got[:, 0], pack[:, 0]]), jnp.stack([pack[:, 0], got[:, 0]])
    ).reshape(4 * NB, W2)
    corner = jnp.where(high, got[:, 1], pack[:, 1]).reshape(W2, W2)

    smem = pl.BlockSpec(memory_space=pltpu.SMEM)
    vmem = pl.BlockSpec(memory_space=pltpu.VMEM)
    weights, low = pl.pallas_call(
        factor_kernel,
        out_shape=(jax.ShapeDtypeStruct((W2, cols), F32), jax.ShapeDtypeStruct((W2, W2), F32)),
        in_specs=[smem, vmem, vmem],
        out_specs=(vmem, vmem),
        name="factor",
    )(q.reshape(1).astype(jnp.int32), corner, lead)

    info = jnp.stack([o.astype(jnp.int32) for o in owners + [core, p, q]])
    whole = lambda shape: pl.BlockSpec(shape, lambda i, s: (0, 0))
    tile = pl.BlockSpec((part, cols), lambda i, s: (s[i], 0))
    out = pl.pallas_call(
        update_kernel,
        out_shape=jax.ShapeDtypeStruct((rows, cols), F32),
        grid_spec=pltpu.PrefetchScalarGridSpec(
            num_scalar_prefetch=1,
            grid=(PIECES,),
            in_specs=[whole((W2, cols)), whole((W2, W2))] + [whole((part, W2))] * 9 + [tile],
            out_specs=tile,
            scratch_shapes=[
                pltpu.VMEM((2 * W2, cols), jnp.bfloat16),
                pltpu.VMEM((W2, cols), jnp.bfloat16),
            ],
        ),
        compiler_params=pltpu.CompilerParams(vmem_limit_bytes=40 * 1024 * 1024),
        name="update",
    )(info, weights, low, *bufs, local)
    return out.reshape(row_blocks, single, nb, cols)


def solution(mesh):
    spec = P(None, "prow", None, "pcol")
    return jax.shard_map(body, mesh=mesh, in_specs=(spec,), out_specs=spec, check_vma=False)
```

time: 678 us -> 111 us (0.16)
  the two profiles are of different devices: /device:TPU:1 before, /device:TPU:32 now
where the time goes in v1:
time: 111 us; the launch traced here: 110 us
  starting transfers between devices  38.8 us (35%)
  waiting for transfers between devices  38.8 us (35%)
  Pallas kernels  19.2 us (17%)
  local copies, waits for them, and re-layouts  7.65 us (7%)
  other arithmetic  5.57 us (5%)
    ppermute x20, starting transfers between devices, over_pcol(): return lax.ppermute(value, AXES, flat)  28.6 us
    ppermute x4, waiting for transfers between devices, over_prow(): return lax.ppermute(value, AXES, flat)  25.2 us
    ppermute x20, waiting for transfers between devices, over_pcol(): return lax.ppermute(value, AXES, flat)  13.6 us
    pallas_call x1, Pallas kernels, body(): pl.pallas_call(factor_kernel, out_shape=(jax.ShapeDtypeStruct((W2, cols),...  13 us
    ppermute x4, starting transfers between devices, over_prow(): return lax.ppermute(value, AXES, flat)  10.2 us
    pallas_call x1, Pallas kernels, body(): pl.pallas_call(update_kernel, out_shape=jax.ShapeDtypeStruct((rows, cols)...  6.2 us
    unnamed x10, local copies, waits for them, and re-layouts  4.53 us
    slice x1, local copies, waits for them, and re-layouts, body(): mine = mine + over_pcol(local[g * part:(g + 1) * part, :W2], [(0, 2 * g)])  3.01 us
  transfers between devices with their start and end apart: 24, of which 5 were waited for; matrix products, arithmetic and copies ran while one was open for 7% of the time, Pallas kernels for 12%

profile of v1, /device:TPU:32, one launch (start us, length us, event | category | flops | bytes accessed | tf_op | source)
XLA Modules:
  0.0 110.4 jit_solution(8343301407566358797)
XLA Ops:
  0.0 0.9 slice_select_fusion.1
  0.9 0.7 collective-permute-start
  1.6 3.0 %fusion.7 = (f32[768,128]{1,0:T(8,128)S(1)}, f32[768,128]{1,0:T(8,128)S(1)}, f32[768,128]{1,0:T(8,128)}, f32[768,128]{1,0:T(8,128)}, f32[768,128]{1,0:T(8,128)}, /*index=5*/f32[768,128]{1,0:T(8,128)}, f32[768,128]{1,0:T(8,128)}) fusion(f32[6144,256]{1,0:T(8,128)} %bitcast.32), kind=kLoop, calls=%fused_computation.21 | loop fusion | bytes 5505024 | tf_op jit(solution)/shard_map/slice | solution.py:139
  4.6 1.3 %collective-permute-start.8 = (f32[768,128]{1,0:T(8,128)S(1)}, f32[768,128]{1,0:T(8,128)S(1)}, u32[]{:S(2)}, u32[]{:S(2)}) collective-permute-start(f32[768,128]{1,0:T(8,128)S(1)} %get-tuple-element.9), channel_id=1, source_target_pairs={{0,2},{16,18},{32,34},{48,50},{64,66},{80,82},{96,98},{112,114},{1... | collective-permute-start | bytes 1179656 | tf_op jit(solution)/shard_map/ppermute | solution.py:26
  5.9 0.7 collective-permute-start.14
  6.6 0.0 collective-permute-done
  6.6 0.9 fusion.8
  7.5 1.3 %collective-permute-start.1 = (f32[256,128]{1,0:T(8,128)S(1)}, f32[256,128]{1,0:T(8,128)S(1)}, u32[]{:S(2)}, u32[]{:S(2)}) collective-permute-start(f32[256,128]{1,0:T(8,128)S(1)} %fusion.8), channel_id=1, source_target_pairs={{0,2},{1,3},{16,18},{17,19},{32,34},{33,35},{48,50},{49,51},{64,66... | collective-permute-start | bytes 393224 | tf_op jit(solution)/shard_map/ppermute | solution.py:26
  8.8 12.5 %collective-permute-done.1 = f32[256,128]{1,0:T(8,128)S(1)} collective-permute-done((f32[256,128]{1,0:T(8,128)S(1)}, f32[256,128]{1,0:T(8,128)S(1)}, u32[]{:S(2)}, u32[]{:S(2)}) %collective-permute-start.1) | collective-permute-done | bytes 131104 | tf_op jit(solution)/shard_map/ppermute | solution.py:26
  21.3 1.3 %collective-permute-start.2 = (f32[256,128]{1,0:T(8,128)S(1)}, f32[256,128]{1,0:T(8,128)S(1)}, u32[]{:S(2)}, u32[]{:S(2)}) collective-permute-start(f32[256,128]{1,0:T(8,128)S(1)} %add.139), channel_id=1, source_target_pairs={{0,4},{1,5},{2,6},{3,7},{16,20},{17,21},{18,22},{19,23},{32,36},{3... | collective-permute-start | bytes 393224 | tf_op jit(solution)/shard_map/ppermute | solution.py:26
  22.6 0.7 collective-permute-start.13
  23.3 0.7 collective-permute-start.12
  24.0 1.1 %collective-permute-done.2 = f32[256,128]{1,0:T(8,128)S(1)} collective-permute-done((f32[256,128]{1,0:T(8,128)S(1)}, f32[256,128]{1,0:T(8,128)S(1)}, u32[]{:S(2)}, u32[]{:S(2)}) %collective-permute-start.2) | collective-permute-done | bytes 131104 | tf_op jit(solution)/shard_map/ppermute | solution.py:26
  25.1 0.7 collective-permute-start.11
  25.8 0.0 collective-permute-done.8
  25.8 0.7 collective-permute-start.10
  26.5 0.0 collective-permute-done.14
  26.5 0.7 collective-permute-start.9
  27.3 0.0 collective-permute-done.13
  27.3 1.3 %collective-permute-start.3 = (f32[256,128]{1,0:T(8,128)S(1)}, f32[256,128]{1,0:T(8,128)S(1)}, u32[]{:S(2)}, u32[]{:S(2)}) collective-permute-start(f32[256,128]{1,0:T(8,128)S(1)} %add.140), channel_id=1, source_target_pairs={{0,8},{1,9},{2,10},{3,11},{4,12},{5,13},{6,14},{7,15},{16,24},{17,... | collective-permute-start | bytes 393224 | tf_op jit(solution)/shard_map/ppermute | solution.py:26
  28.6 0.0 collective-permute-done.12
  28.6 0.0 collective-permute-done.11
  28.6 0.0 collective-permute-done.10
  28.6 0.0 collective-permute-done.9
  28.6 1.1 %fusion.6 = f32[768,128]{1,0:T(8,128)S(1)} fusion(f32[768,128]{1,0:T(8,128)S(1)} %collective-permute-done.14, f32[768,128]{1,0:T(8,128)S(1)} %collective-permute-done.13, f32[768,128]{1,0:T(8,128)S(1)} %collective-permute-done.12, f32[768,128]{1,0:T(8,128)S(1)} %collective-permute-done.11, f32[768,128]{1,0:T(8,128)S(1)} %collective-permute-done.10, ...), kind=kLoop, calls=%fused_computation.7 | loop fusion | flops 786432 | bytes 3538945 | tf_op jit(solution)/shard_map/add | solution.py:139
  29.8 1.3 %collective-permute-start.15 = (f32[768,128]{1,0:T(8,128)S(1)}, f32[768,128]{1,0:T(8,128)S(1)}, u32[]{:S(2)}, u32[]{:S(2)}) collective-permute-start(f32[768,128]{1,0:T(8,128)S(1)} %fusion.6), channel_id=1, source_target_pairs={{0,1},{2,3},{4,5},{6,7},{8,9},{10,11},{12,13},{14,15},{16,17},{18,... | collective-permute-start | bytes 1179656 | tf_op jit(solution)/shard_map/ppermute | solution.py:26
  31.1 0.0 collective-permute-done.3
  31.2 1.7 %collective-permute-start.4 = (f32[2,64,128]{2,1,0:T(8,128)S(1)}, f32[2,64,128]{2,1,0:T(8,128)S(1)}, u32[]{:S(2)}, u32[]{:S(2)}) collective-permute-start(f32[2,64,128]{2,1,0:T(8,128)S(1)} %pad_maximum_fusion), channel_id=1, source_target_pairs={{0,64},{16,80},{32,96},{48,112},{64,0},{80,16},{96,32},{112,48},{1... | collective-permute-start | bytes 196616 | tf_op jit(solution)/shard_map/ppermute | solution.py:31
  32.8 0.1 pad_add_fusion.1
  32.9 2.6 %collective-permute-done.4 = f32[2,64,128]{2,1,0:T(8,128)S(1)} collective-permute-done((f32[2,64,128]{2,1,0:T(8,128)S(1)}, f32[2,64,128]{2,1,0:T(8,128)S(1)}, u32[]{:S(2)}, u32[]{:S(2)}) %collective-permute-start.4) | collective-permute-done | bytes 65568 | tf_op jit(solution)/shard_map/ppermute | solution.py:31
  35.5 0.1 broadcast_select_fusion
  35.6 3.2 %collective-permute-start.5 = (f32[2,64,128]{2,1,0:T(8,128)S(1)}, f32[2,64,128]{2,1,0:T(8,128)S(1)}, u32[]{:S(2)}, u32[]{:S(2)}) collective-permute-start(f32[2,64,128]{2,1,0:T(8,128)S(1)} %broadcast_select_fusion), channel_id=1, source_target_pairs={{0,128},{16,144},{32,160},{48,176},{64,192},{80,208},{96,224},{112... | collective-permute-start | bytes 196616 | tf_op jit(solution)/shard_map/ppermute | solution.py:31
  38.8 0.1 pad_add_fusion
  38.9 14.1 %collective-permute-start.16 = (f32[768,128]{1,0:T(8,128)S(1)}, f32[768,128]{1,0:T(8,128)S(1)}, u32[]{:S(2)}, u32[]{:S(2)}) collective-permute-start(f32[768,128]{1,0:T(8,128)S(1)} %fusion.6), channel_id=1, source_target_pairs={{0,10},{2,8},{4,14},{6,12},{8,2},{10,0},{12,6},{14,4},{16,26},{18,... | collective-permute-start | bytes 1179656 | tf_op jit(solution)/shard_map/ppermute | solution.py:26
  52.9 0.0 collective-permute-done.15
  53.0 0.1 collective-permute-start.22
  53.1 0.1 collective-permute-start.20
  53.2 2.0 %collective-permute-start.18 = (f32[768,128]{1,0:T(8,128)S(1)}, f32[768,128]{1,0:T(8,128)S(1)}, u32[]{:S(2)}, u32[]{:S(2)}) collective-permute-start(f32[768,128]{1,0:T(8,128)S(1)} %add.150.refs_0_), channel_id=1, source_target_pairs={{0,4},{2,6},{4,8},{6,10},{8,12},{10,14},{12,0},{14,2},{1,13},{3,15... | collective-permute-start | bytes 1179656 | tf_op jit(solution)/shard_map/ppermute | solution.py:26
  55.2 0.0 collective-permute-done.5
  55.2 0.1 broadcast_select_fusion.1
  55.3 3.4 %collective-permute-start.6 = (f32[2,64,128]{2,1,0:T(8,128)S(1)}, f32[2,64,128]{2,1,0:T(8,128)S(1)}, u32[]{:S(2)}, u32[]{:S(2)}) collective-permute-start(f32[2,64,128]{2,1,0:T(8,128)S(1)} %broadcast_select_fusion.1), channel_id=1, source_target_pairs={{0,16},{16,0},{32,48},{48,32},{64,80},{80,64},{96,112},{112,96},{1... | collective-permute-start | bytes 196616 | tf_op jit(solution)/shard_map/ppermute | solution.py:31
  58.7 0.1 stack.94.info
  58.8 16.3 %collective-permute-done.6 = f32[2,64,128]{2,1,0:T(8,128)S(1)} collective-permute-done((f32[2,64,128]{2,1,0:T(8,128)S(1)}, f32[2,64,128]{2,1,0:T(8,128)S(1)}, u32[]{:S(2)}, u32[]{:S(2)}) %collective-permute-start.6) | collective-permute-done | bytes 65568 | tf_op jit(solution)/shard_map/ppermute | solution.py:31
  75.1 2.0 %collective-permute-start.7 = (f32[2,2,64,128]{3,2,0,1:T(8,128)S(1)}, f32[2,2,64,128]{3,2,0,1:T(8,128)S(1)}, u32[]{:S(2)}, u32[]{:S(2)}) collective-permute-start(f32[2,2,64,128]{3,2,0,1:T(8,128)S(1)} %copy.2), channel_id=1, source_target_pairs={{0,32},{16,48},{32,0},{48,16},{64,96},{80,112},{96,64},{112,80},{1... | collective-permute-start | bytes 393224 | tf_op jit(solution)/shard_map/ppermute | solution.py:31
  77.1 0.0 collective-permute-done.16.refs_1_
  77.1 0.0 collective-permute-start.17
  77.1 0.0 collective-permute-done.22.refs_7_
  77.1 0.6 collective-permute-start.23
  77.7 0.0 collective-permute-done.20.refs_5_
  77.7 0.1 collective-permute-start.21
  77.8 0.0 collective-permute-done.18.refs_3_
  77.8 0.4 collective-permute-start.19
  78.2 6.3 %collective-permute-done.7 = f32[2,2,64,128]{3,2,0,1:T(8,128)S(1)} collective-permute-done((f32[2,2,64,128]{3,2,0,1:T(8,128)S(1)}, f32[2,2,64,128]{3,2,0,1:T(8,128)S(1)}, u32[]{:S(2)}, u32[]{:S(2)}) %collective-permute-start.7) | collective-permute-done | bytes 131104 | tf_op jit(solution)/shard_map/ppermute | solution.py:31
  84.5 1.5 %slice_bitcast_fusion.1 = (f32[1,2,64,128]{3,2,1,0:T(8,128)S(1)}, f32[2,1,64,128]{3,2,0,1:T(8,128)}) fusion(f32[2,2,64,128]{3,2,0,1:T(8,128)S(1)} %collective-permute-done.7, pred[]{:T(512)S(6)} %ge.6, f32[1,2,64,128]{3,2,1,0:T(8,128)} %bitcast.37, f32[1,2,64,128]{3,2,1,0:T(8,128)} %bitcast.41, pred[]{:T(512)S(6)} %eq.40), kind=kLoop, calls=%fused_computation.12 | loop fusion | flops 114688 | bytes 393218 | tf_op jit(solution)/shard_map/stack;squeeze | solution.py:170
  86.0 0.7 maximum_select_fusion.1
  86.7 13.0 %factor.1 = (f32[128,256]{1,0:T(8,128)}, f32[128,128]{1,0:T(8,128)}) custom-call(s32[1]{0:T(128)} %bitcast.10.q_ref, f32[128,128]{1,0:T(8,128)} %bitcast.39, f32[256,128]{1,0:T(8,128)} %bitcast.38), custom_call_target="tpu_custom_call" | custom-call | tf_op jit(solution)/shard_map/factor/pallas_call | solution.py:176
  99.6 0.0 collective-permute-done.17.refs_2_
  99.6 0.0 collective-permute-done.23.refs_8_
  99.7 0.0 collective-permute-done.19.refs_4_
  99.7 0.0 copy-start
  99.7 2.8 %copy-done = f32[96,1,64,256]{3,2,1,0:T(8,128)S(1)} copy-done((f32[96,1,64,256]{3,2,1,0:T(8,128)S(1)}, f32[96,1,64,256]{3,2,1,0:T(8,128)}, u32[]{:S(2)}) %copy-start) | copy-done | bytes 6291480
  102.5 0.9 copy-done.1
  103.4 0.8 copy-done.2
  104.2 6.2 %update.1 = f32[6144,256]{1,0:T(8,128)} custom-call(s32[11]{0:T(128)S(1)} %stack.94.info, f32[128,256]{1,0:T(8,128)S(1)} %copy-done.1, f32[128,128]{1,0:T(8,128)S(1)} %copy-done.2, f32[768,128]{1,0:T(8,128)S(1)} %add.150.refs_0_, f32[768,128]{1,0:T(8,128)S(1)} %collective-permute-done.16.refs_1_, f32[768,128]{1,0:T(8,128)S(1)} %collective-permute-done.17.refs_2_, ...), custom_call_target="tpu_custom_call" | custom-call | tf_op jit(solution)/shard_map/update/pallas_call | solution.py:187
  (16 shorter events, 0.2 us)
Async XLA Ops:
  0.9 5.7 %collective-permute-start = (f32[256,128]{1,0:T(8,128)S(1)}, f32[256,128]{1,0:T(8,128)S(1)}, u32[]{:S(2)}, u32[]{:S(2)}) collective-permute-start(f32[256,128]{1,0:T(8,128)S(1)} %slice_select_fusion.1), channel_id=1, source_target_pairs={{0,1},{16,17},{32,33},{48,49},{64,65},{80,81},{96,97},{112,113},{1... | collective-permute-start | bytes 393224 | tf_op jit(solution)/shard_map/ppermute | solution.py:26
  4.6 21.2 %collective-permute-start.8 = (f32[768,128]{1,0:T(8,128)S(1)}, f32[768,128]{1,0:T(8,128)S(1)}, u32[]{:S(2)}, u32[]{:S(2)}) collective-permute-start(f32[768,128]{1,0:T(8,128)S(1)} %get-tuple-element.9), channel_id=1, source_target_pairs={{0,2},{16,18},{32,34},{48,50},{64,66},{80,82},{96,98},{112,114},{1... | collective-permute-start | bytes 1179656 | tf_op jit(solution)/shard_map/ppermute | solution.py:26
  5.9 20.6 %collective-permute-start.14 = (f32[768,128]{1,0:T(8,128)S(1)}, f32[768,128]{1,0:T(8,128)S(1)}, u32[]{:S(2)}, u32[]{:S(2)}) collective-permute-start(f32[768,128]{1,0:T(8,128)S(1)} %get-tuple-element.10), channel_id=1, source_target_pairs={{0,14},{16,30},{32,46},{48,62},{64,78},{80,94},{96,110},{112,126},... | collective-permute-start | bytes 1179656 | tf_op jit(solution)/shard_map/ppermute | solution.py:26
  7.5 13.8 %collective-permute-start.1 = (f32[256,128]{1,0:T(8,128)S(1)}, f32[256,128]{1,0:T(8,128)S(1)}, u32[]{:S(2)}, u32[]{:S(2)}) collective-permute-start(f32[256,128]{1,0:T(8,128)S(1)} %fusion.8), channel_id=1, source_target_pairs={{0,2},{1,3},{16,18},{17,19},{32,34},{33,35},{48,50},{49,51},{64,66... | collective-permute-start | bytes 393224 | tf_op jit(solution)/shard_map/ppermute | solution.py:26
  21.3 3.8 %collective-permute-start.2 = (f32[256,128]{1,0:T(8,128)S(1)}, f32[256,128]{1,0:T(8,128)S(1)}, u32[]{:S(2)}, u32[]{:S(2)}) collective-permute-start(f32[256,128]{1,0:T(8,128)S(1)} %add.139), channel_id=1, source_target_pairs={{0,4},{1,5},{2,6},{3,7},{16,20},{17,21},{18,22},{19,23},{32,36},{3... | collective-permute-start | bytes 393224 | tf_op jit(solution)/shard_map/ppermute | solution.py:26
  22.6 4.7 %collective-permute-start.13 = (f32[768,128]{1,0:T(8,128)}, f32[768,128]{1,0:T(8,128)S(1)}, u32[]{:S(2)}, u32[]{:S(2)}) collective-permute-start(f32[768,128]{1,0:T(8,128)} %get-tuple-element.11), channel_id=1, source_target_pairs={{0,12},{16,28},{32,44},{48,60},{64,76},{80,92},{96,108},{112,124},... | collective-permute-start | bytes 1179656 | tf_op jit(solution)/shard_map/ppermute | solution.py:26
  23.3 5.3 %collective-permute-start.12 = (f32[768,128]{1,0:T(8,128)}, f32[768,128]{1,0:T(8,128)S(1)}, u32[]{:S(2)}, u32[]{:S(2)}) collective-permute-start(f32[768,128]{1,0:T(8,128)} %get-tuple-element.12), channel_id=1, source_target_pairs={{0,10},{16,26},{32,42},{48,58},{64,74},{80,90},{96,106},{112,122},... | collective-permute-start | bytes 1179656 | tf_op jit(solution)/shard_map/ppermute | solution.py:26
  25.1 3.5 %collective-permute-start.11 = (f32[768,128]{1,0:T(8,128)}, f32[768,128]{1,0:T(8,128)S(1)}, u32[]{:S(2)}, u32[]{:S(2)}) collective-permute-start(f32[768,128]{1,0:T(8,128)} %get-tuple-element.13), channel_id=1, source_target_pairs={{0,8},{16,24},{32,40},{48,56},{64,72},{80,88},{96,104},{112,120},{... | collective-permute-start | bytes 1179656 | tf_op jit(solution)/shard_map/ppermute | solution.py:26
  25.8 2.8 %collective-permute-start.10 = (f32[768,128]{1,0:T(8,128)}, f32[768,128]{1,0:T(8,128)S(1)}, u32[]{:S(2)}, u32[]{:S(2)}) collective-permute-start(f32[768,128]{1,0:T(8,128)} %get-tuple-element.14), channel_id=1, source_target_pairs={{0,6},{16,22},{32,38},{48,54},{64,70},{80,86},{96,102},{112,118},{... | collective-permute-start | bytes 1179656 | tf_op jit(solution)/shard_map/ppermute | solution.py:26
  26.5 2.1 %collective-permute-start.9 = (f32[768,128]{1,0:T(8,128)}, f32[768,128]{1,0:T(8,128)S(1)}, u32[]{:S(2)}, u32[]{:S(2)}) collective-permute-start(f32[768,128]{1,0:T(8,128)} %get-tuple-element.15), channel_id=1, source_target_pairs={{0,4},{16,20},{32,36},{48,52},{64,68},{80,84},{96,100},{112,116},{... | collective-permute-start | bytes 1179656 | tf_op jit(solution)/shard_map/ppermute | solution.py:26
  27.3 3.8 %collective-permute-start.3 = (f32[256,128]{1,0:T(8,128)S(1)}, f32[256,128]{1,0:T(8,128)S(1)}, u32[]{:S(2)}, u32[]{:S(2)}) collective-permute-start(f32[256,128]{1,0:T(8,128)S(1)} %add.140), channel_id=1, source_target_pairs={{0,8},{1,9},{2,10},{3,11},{4,12},{5,13},{6,14},{7,15},{16,24},{17,... | collective-permute-start | bytes 393224 | tf_op jit(solution)/shard_map/ppermute | solution.py:26
  29.8 23.2 %collective-permute-start.15 = (f32[768,128]{1,0:T(8,128)S(1)}, f32[768,128]{1,0:T(8,128)S(1)}, u32[]{:S(2)}, u32[]{:S(2)}) collective-permute-start(f32[768,128]{1,0:T(8,128)S(1)} %fusion.6), channel_id=1, source_target_pairs={{0,1},{2,3},{4,5},{6,7},{8,9},{10,11},{12,13},{14,15},{16,17},{18,... | collective-permute-start | bytes 1179656 | tf_op jit(solution)/shard_map/ppermute | solution.py:26
  31.2 4.4 %collective-permute-start.4 = (f32[2,64,128]{2,1,0:T(8,128)S(1)}, f32[2,64,128]{2,1,0:T(8,128)S(1)}, u32[]{:S(2)}, u32[]{:S(2)}) collective-permute-start(f32[2,64,128]{2,1,0:T(8,128)S(1)} %pad_maximum_fusion), channel_id=1, source_target_pairs={{0,64},{16,80},{32,96},{48,112},{64,0},{80,16},{96,32},{112,48},{1... | collective-permute-start | bytes 196616 | tf_op jit(solution)/shard_map/ppermute | solution.py:31
  35.6 19.6 %collective-permute-start.5 = (f32[2,64,128]{2,1,0:T(8,128)S(1)}, f32[2,64,128]{2,1,0:T(8,128)S(1)}, u32[]{:S(2)}, u32[]{:S(2)}) collective-permute-start(f32[2,64,128]{2,1,0:T(8,128)S(1)} %broadcast_select_fusion), channel_id=1, source_target_pairs={{0,128},{16,144},{32,160},{48,176},{64,192},{80,208},{96,224},{112... | collective-permute-start | bytes 196616 | tf_op jit(solution)/shard_map/ppermute | solution.py:31
  38.9 38.2 %collective-permute-start.16 = (f32[768,128]{1,0:T(8,128)S(1)}, f32[768,128]{1,0:T(8,128)S(1)}, u32[]{:S(2)}, u32[]{:S(2)}) collective-permute-start(f32[768,128]{1,0:T(8,128)S(1)} %fusion.6), channel_id=1, source_target_pairs={{0,10},{2,8},{4,14},{6,12},{8,2},{10,0},{12,6},{14,4},{16,26},{18,... | collective-permute-start | bytes 1179656 | tf_op jit(solution)/shard_map/ppermute | solution.py:26
  53.0 24.1 %collective-permute-start.22 = (f32[768,128]{1,0:T(8,128)S(1)}, f32[768,128]{1,0:T(8,128)S(1)}, u32[]{:S(2)}, u32[]{:S(2)}) collective-permute-start(f32[768,128]{1,0:T(8,128)S(1)} %add.150.refs_0_), channel_id=1, source_target_pairs={{0,6},{2,4},{4,10},{6,8},{8,14},{10,12},{12,2},{14,0},{1,15},{3,13... | collective-permute-start | bytes 1179656 | tf_op jit(solution)/shard_map/ppermute | solution.py:26
  53.1 24.6 %collective-permute-start.20 = (f32[768,128]{1,0:T(8,128)S(1)}, f32[768,128]{1,0:T(8,128)S(1)}, u32[]{:S(2)}, u32[]{:S(2)}) collective-permute-start(f32[768,128]{1,0:T(8,128)S(1)} %add.150.refs_0_), channel_id=1, source_target_pairs={{0,2},{2,0},{4,6},{6,4},{8,10},{10,8},{12,14},{14,12},{1,9},{3,11}... | collective-permute-start | bytes 1179656 | tf_op jit(solution)/shard_map/ppermute | solution.py:26
  53.2 24.6 %collective-permute-start.18 = (f32[768,128]{1,0:T(8,128)S(1)}, f32[768,128]{1,0:T(8,128)S(1)}, u32[]{:S(2)}, u32[]{:S(2)}) collective-permute-start(f32[768,128]{1,0:T(8,128)S(1)} %add.150.refs_0_), channel_id=1, source_target_pairs={{0,4},{2,6},{4,8},{6,10},{8,12},{10,14},{12,0},{14,2},{1,13},{3,15... | collective-permute-start | bytes 1179656 | tf_op jit(solution)/shard_map/ppermute | solution.py:26
  55.3 21.8 %copy-start.3 = (f32[2,64,128]{2,1,0:T(8,128)}, f32[2,64,128]{2,1,0:T(8,128)S(1)}, u32[]{:S(2)}) copy-start(f32[2,64,128]{2,1,0:T(8,128)S(1)} %broadcast_select_fusion.1) | copy-start | bytes 196612
  55.3 19.8 %collective-permute-start.6 = (f32[2,64,128]{2,1,0:T(8,128)S(1)}, f32[2,64,128]{2,1,0:T(8,128)S(1)}, u32[]{:S(2)}, u32[]{:S(2)}) collective-permute-start(f32[2,64,128]{2,1,0:T(8,128)S(1)} %broadcast_select_fusion.1), channel_id=1, source_target_pairs={{0,16},{16,0},{32,48},{48,32},{64,80},{80,64},{96,112},{112,96},{1... | collective-permute-start | bytes 196616 | tf_op jit(solution)/shard_map/ppermute | solution.py:31
  75.1 2.0 %copy-start.4 = (f32[2,64,128]{2,1,0:T(8,128)}, f32[2,64,128]{2,1,0:T(8,128)S(1)}, u32[]{:S(2)}) copy-start(f32[2,64,128]{2,1,0:T(8,128)S(1)} %collective-permute-done.6) | copy-start | bytes 196612
  75.1 9.3 %collective-permute-start.7 = (f32[2,2,64,128]{3,2,0,1:T(8,128)S(1)}, f32[2,2,64,128]{3,2,0,1:T(8,128)S(1)}, u32[]{:S(2)}, u32[]{:S(2)}) collective-permute-start(f32[2,2,64,128]{3,2,0,1:T(8,128)S(1)} %copy.2), channel_id=1, source_target_pairs={{0,32},{16,48},{32,0},{48,16},{64,96},{80,112},{96,64},{112,80},{1... | collective-permute-start | bytes 393224 | tf_op jit(solution)/shard_map/ppermute | solution.py:31
  77.1 22.5 %collective-permute-start.17 = (f32[768,128]{1,0:T(8,128)S(1)}, f32[768,128]{1,0:T(8,128)S(1)}, u32[]{:S(2)}, u32[]{:S(2)}) collective-permute-start(f32[768,128]{1,0:T(8,128)S(1)} %collective-permute-done.16.refs_1_), channel_id=1, source_target_pairs={{0,1},{1,0},{2,3},{3,2},{4,5},{5,4},{6,7},{7,6},{8,9},{9,8},{10,11... | collective-permute-start | bytes 1179656 | tf_op jit(solution)/shard_map/ppermute | solution.py:26
  77.1 22.5 %collective-permute-start.23 = (f32[768,128]{1,0:T(8,128)S(1)}, f32[768,128]{1,0:T(8,128)S(1)}, u32[]{:S(2)}, u32[]{:S(2)}) collective-permute-start(f32[768,128]{1,0:T(8,128)S(1)} %collective-permute-done.22.refs_7_), channel_id=1, source_target_pairs={{0,1},{1,0},{2,3},{3,2},{4,5},{5,4},{6,7},{7,6},{8,9},{9,8},{10,11... | collective-permute-start | bytes 1179656 | tf_op jit(solution)/shard_map/ppermute | solution.py:26
  77.7 21.9 %collective-permute-start.21 = (f32[768,128]{1,0:T(8,128)S(1)}, f32[768,128]{1,0:T(8,128)S(1)}, u32[]{:S(2)}, u32[]{:S(2)}) collective-permute-start(f32[768,128]{1,0:T(8,128)S(1)} %collective-permute-done.20.refs_5_), channel_id=1, source_target_pairs={{0,1},{1,0},{2,3},{3,2},{4,5},{5,4},{6,7},{7,6},{8,9},{9,8},{10,11... | collective-permute-start | bytes 1179656 | tf_op jit(solution)/shard_map/ppermute | solution.py:26
  77.8 21.8 %collective-permute-start.19 = (f32[768,128]{1,0:T(8,128)S(1)}, f32[768,128]{1,0:T(8,128)S(1)}, u32[]{:S(2)}, u32[]{:S(2)}) collective-permute-start(f32[768,128]{1,0:T(8,128)S(1)} %collective-permute-done.18.refs_3_), channel_id=1, source_target_pairs={{0,1},{1,0},{2,3},{3,2},{4,5},{5,4},{6,7},{7,6},{8,9},{9,8},{10,11... | collective-permute-start | bytes 1179656 | tf_op jit(solution)/shard_map/ppermute | solution.py:26
  99.7 2.8 %copy-start = (f32[96,1,64,256]{3,2,1,0:T(8,128)S(1)}, f32[96,1,64,256]{3,2,1,0:T(8,128)}, u32[]{:S(2)}) copy-start(f32[96,1,64,256]{3,2,1,0:T(8,128)} %param.1) | copy-start | bytes 18874372
  102.5 0.9 copy-start.1
  103.4 0.8 copy-start.2

commit v2 on v0

v2 whole, which is shorter than its diff:
```python
import functools

import jax
import jax.numpy as jnp
from jax import lax
from jax.experimental import pallas as pl
from jax.experimental.pallas import tpu as pltpu
from jax.sharding import PartitionSpec as P

AXES = ("prow", "pcol")
NP, NQ = 16, 16
NB = 64
W2 = 2 * NB
PIECES = 8
F32 = jnp.float32
BF16 = jnp.bfloat16
HI = lax.Precision.HIGHEST


def chip_move(chip, dx, dz):
    x, z = chip // 2, chip % 2
    return ((x + dx) % 4) * 2 + (z + dz) % 2


def over_pcol(value, pairs):
    flat = [(p * NQ + s, p * NQ + d) for p in range(NP) for s, d in pairs]
    return lax.ppermute(value, AXES, flat)


def over_prow(value, pairs):
    flat = [(s * NQ + q, d * NQ + q) for q in range(NQ) for s, d in pairs]
    return lax.ppermute(value, AXES, flat)


def factor(raw):
    r = lax.broadcasted_iota(jnp.int32, (W2, W2), 0)
    c = lax.broadcasted_iota(jnp.int32, (W2, W2), 1)
    low = jnp.where(r >= c, raw, 0.0)
    sym = jnp.where(r >= c, low, low.T)
    eye = jnp.where(r == c, 1.0, 0.0).astype(F32)
    nt = W2 // 8
    left = [sym[8 * t : 8 * t + 8] for t in range(nt)]
    right = [eye[8 * t : 8 * t + 8] for t in range(nt)]
    sub = lax.broadcasted_iota(jnp.int32, (8, W2), 0)
    up, inv_rows = [], []
    for k in range(nt):
        cols = {}
        for t in range(k, nt):
            for j in range(8):
                a = left[t][:, 8 * k + j : 8 * k + j + 1]
                cols[t, j] = jnp.broadcast_to(a, (8, W2))
        for s in range(8):
            inv = lax.rsqrt(cols[k, s][s : s + 1])
            lrow = left[k][s : s + 1] * inv
            rrow = right[k][s : s + 1] * inv
            up.append(lrow)
            inv_rows.append(rrow)
            pivots = {j: cols[k, j][s : s + 1] * inv for j in range(s + 1, 8)}
            for t in range(k, nt):
                f = cols[t, s] * inv
                if t == k:
                    f = jnp.where(sub > s, f, 0.0)
                for j in range(s + 1, 8):
                    cols[t, j] = cols[t, j] - f * pivots[j]
                left[t] = left[t] - f * lrow
                right[t] = right[t] - f * rrow
    upper = jnp.where(r <= c, jnp.concatenate(up, axis=0), 0.0)
    linv = jnp.where(r >= c, jnp.concatenate(inv_rows, axis=0), 0.0)
    return upper.T, linv, eye


def pack_kernel(chips, local, *refs):
    outs, sem = refs[:-1], refs[-1]
    part = outs[0].shape[0] - W2
    copies = []
    for k, g in enumerate(chips):
        for j, (src, dst, n) in enumerate(
            ((g * part, 0, part), (0, part, NB), (g // 2 * NB, part + NB, NB))
        ):
            copies.append(
                pltpu.make_async_copy(
                    local.at[pl.ds(src, n), pl.ds(0, W2)], outs[k].at[pl.ds(dst, n)], sem.at[k, j]
                )
            )
    for copy in copies:
        copy.start()
    for copy in copies:
        copy.wait()


def finish_kernel(
    info, corner_ref, lead_ref, *refs
):
    bufs, state, out = refs[:9], refs[9], refs[10]
    x_v, s_v, o_v, mhh, mlo, low_v, x_sem, s_sem, o_sem = refs[11:]
    rows, cols = s_v.shape[1:]
    core, p, q = info[8], info[9], info[10]

    def place(k):
        return pl.ds(pl.multiple_of(info[k] * rows, rows), rows)

    def load_s(k):
        return pltpu.make_async_copy(state.at[place(k)], s_v.at[k], s_sem.at[k])

    def load_x(k, ref):
        return pltpu.make_async_copy(ref, x_v.at[k], x_sem.at[k])

    def store(k):
        return pltpu.make_async_copy(o_v.at[k], out.at[place(k)], o_sem.at[k])

    for k in range(PIECES):
        load_s(k).start()
    load_x(0, bufs[0]).start()

    @pl.when(core == 0)
    def _():
        load_x(1, bufs[1]).start()

    @pl.when(core == 1)
    def _():
        load_x(1, bufs[2]).start()

    for k in range(2, PIECES):
        load_x(k, bufs[k + 1]).start()

    low, linv, eye = factor(corner_ref[...])
    low_v[...] = low
    y = lax.dot_general(
        linv, lead_ref[...], (((1,), (1,)), ((), ())), precision=HI, preferred_element_type=F32
    )
    y = jnp.concatenate([jnp.where(q == 0, -eye, y[:, :W2]), y[:, W2:]], axis=1)
    m = lax.dot_general(
        linv, y, (((0,), (0,)), ((), ())), precision=HI, preferred_element_type=F32
    )
    hi = m.astype(BF16)
    mhh[0:W2] = hi
    mhh[W2 : 2 * W2] = hi
    mlo[...] = (m - hi.astype(F32)).astype(BF16)

    def piece(k, carry):
        load_s(k).wait()
        load_x(k, bufs[0]).wait()
        x = x_v[k]
        xh = x.astype(BF16)
        xl = (x - xh.astype(F32)).astype(BF16)
        prod = jnp.dot(jnp.concatenate([xh, xl], axis=1), mhh[...], preferred_element_type=F32)
        prod += jnp.dot(xh, mlo[...], preferred_element_type=F32)
        lane = lax.broadcasted_iota(jnp.int32, (1, cols), 1)
        replaced = (q == 0) & (lane < W2)
        o_v[k] = jnp.where(replaced, 0.0, s_v[k]) - prod

        @pl.when(info[k] == 0)
        def _():
            top = 4 * NB
            rr = lax.broadcasted_iota(jnp.int32, (top, cols), 0)
            cc = lax.broadcasted_iota(jnp.int32, (top, cols), 1) + q * cols
            rg = ((rr // NB) * NP + p) * NB + rr % NB
            o_v[k, 0:top] = jnp.where(rg >= cc, o_v[k, 0:top], s_v[k, 0:top])

        @pl.when((info[k] == 0) & (q == 0) & (p < 2))
        def _():
            rr = lax.broadcasted_iota(jnp.int32, (NB, W2), 0) + p * NB
            cc = lax.broadcasted_iota(jnp.int32, (NB, W2), 1)
            part = low_v[pl.ds(pl.multiple_of(jnp.minimum(p, 1) * NB, NB), NB), :]
            o_v[k, 0:NB, 0:W2] = jnp.where(rr >= cc, part, s_v[k, 0:NB, 0:W2])

        store(k).start()
        return carry

    lax.fori_loop(0, PIECES, piece, 0)
    for k in range(PIECES):
        store(k).wait()


def body(covariance):
    row_blocks, single, nb, cols = covariance.shape
    rows = row_blocks * nb
    local = covariance.reshape(rows, cols)
    p = lax.axis_index("prow")
    q = lax.axis_index("pcol")
    y, z = p // 4, p % 4
    chip, core = q // 2, q % 2
    part = rows // PIECES
    is_src = q == 0
    smem = pl.BlockSpec(memory_space=pltpu.SMEM)
    vmem = pl.BlockSpec(memory_space=pltpu.VMEM)
    hbm = pl.BlockSpec(memory_space=pl.ANY)

    messages = {}
    for chips in ((3, 7, 5), (4, 6, 1, 2, 0)):
        got = pl.pallas_call(
            functools.partial(pack_kernel, chips),
            out_shape=[jax.ShapeDtypeStruct((part + W2, W2), F32)] * len(chips),
            in_specs=[hbm],
            out_specs=[vmem] * len(chips),
            scratch_shapes=[pltpu.SemaphoreType.DMA((len(chips), 3))],
            name="pack",
        )(local)
        messages.update(zip(chips, got))
    relay = over_pcol(messages[3], [(0, 5)]) + over_pcol(messages[7], [(0, 13)])
    mine = jnp.where(is_src, messages[0], 0.0)
    for g in (5, 4, 6, 1, 2):
        mine = mine + over_pcol(messages[g], [(0, 2 * g)])
    mine = mine + over_pcol(relay, [(5, 6), (13, 14)])
    lend = [(2 * g, 2 * g + 1) for g in range(PIECES)]
    mine = mine + over_pcol(mine, lend)
    both = mine[:part]
    pack = mine[part:].reshape(2, NB, W2)

    root = q % 4
    got = over_prow(pack, [(s, s ^ 4) for s in range(NP)])
    pack = jnp.stack([jnp.where(y == 1, got[0], pack[0]), jnp.where(y == root ^ 1, got[1], pack[1])])
    got = over_prow(pack, [(s, s ^ 12) for s in range(NP)])
    pack = jnp.stack(
        [jnp.where(y >= 2, got[0], pack[0]), jnp.where(y // 2 != root // 2, got[1], pack[1])]
    )
    got = over_prow(pack, [(s, s ^ 1) for s in range(NP)])
    odd = z % 2 == 1
    pack = jnp.where(odd, jnp.stack([got, pack], 1), jnp.stack([pack, got], 1))
    got = over_prow(pack, [(s, s ^ 3) for s in range(NP)])
    high = z >= 2
    corner = jnp.where(high, got[0], pack[0]).reshape(W2, W2)
    lead = jnp.concatenate(
        [jnp.where(high, got, pack)[1], jnp.where(high, pack, got)[1]]
    ).reshape(4 * NB, W2)

    swap = [(s, s ^ 1) for s in range(NQ)]

    def send(value, m0, m1):
        pairs = [(2 * g, 2 * chip_move(g, *m0)) for g in range(PIECES)]
        if m1 is not None:
            pairs += [(2 * g + 1, 2 * chip_move(g, *m1) + 1) for g in range(PIECES)]
        return over_pcol(value, pairs)

    def owner(m0, m1):
        own = [((chip // 2 - m[0]) % 4) * 2 + (chip + m[1]) % 2 for m in (m0, m1)]
        return [jnp.where(core == 0, own[0], own[1]), jnp.where(core == 0, own[1], own[0])]

    side = send(both, (1, 0), (-1, 0))
    later = both
    cross = send(later, (1, 1), (-1, 1))
    over = send(later, (0, 1), None)
    again = send(jnp.where(core == 0, side, cross), (1, 0), (-1, 0))
    bufs = [both, over, over_pcol(over, lend)]
    owners = [chip, chip // 2 * 2 + 1 - chip % 2]
    for got, moves in (
        (side, ((1, 0), (-1, 0))),
        (cross, ((1, 1), (-1, 1))),
        (again, ((2, 0), (-2, 1))),
    ):
        bufs += [got, over_pcol(got, swap)]
        owners += owner(*moves)

    info = jnp.stack([o.astype(jnp.int32) for o in owners + [core, p, q]])
    out = pl.pallas_call(
        finish_kernel,
        out_shape=jax.ShapeDtypeStruct((rows, cols), F32),
        in_specs=[smem, vmem, vmem] + [hbm] * 10,
        out_specs=hbm,
        scratch_shapes=[
            pltpu.VMEM((PIECES, part, W2), F32),
            pltpu.VMEM((PIECES, part, cols), F32),
            pltpu.VMEM((PIECES, part, cols), F32),
            pltpu.VMEM((2 * W2, cols), BF16),
            pltpu.VMEM((W2, cols), BF16),
            pltpu.VMEM((W2, W2), F32),
            pltpu.SemaphoreType.DMA((PIECES,)),
            pltpu.SemaphoreType.DMA((PIECES,)),
            pltpu.SemaphoreType.DMA((PIECES,)),
        ],
        compiler_params=pltpu.CompilerParams(vmem_limit_bytes=52 * 1024 * 1024),
        name="finish",
    )(info, corner, lead, *bufs, local)
    return out.reshape(row_blocks, single, nb, cols)


def solution(mesh):
    spec = P(None, "prow", None, "pcol")
    return jax.shard_map(body, mesh=mesh, in_specs=(spec,), out_specs=spec, check_vma=False)
```

time: 678 us -> 73.6 us (0.11)
  waiting for transfers between devices: 399 us -> 28.3 us
  blocking collectives: 138 us -> 0 us
  local copies, waits for them, and re-layouts: 59 us -> 0.88 us
  other arithmetic: 38.1 us -> 1.17 us
  matrix products: 27.9 us -> 0 us
  starting transfers between devices: 0.13 us -> 26.4 us
  Pallas kernels: 0 us -> 15.9 us
  between operations: 13.3 us -> 0.49 us
    psum x2 -> x0, waiting for transfers between devices: 284 us -> none  [broadcast(): return lax.psum(kept, axis)]
    psum x2 -> x0, blocking collectives: 138 us -> none  [broadcast(): return lax.psum(kept, axis)]
    all_gather x2 -> x0, waiting for transfers between devices: 116 us -> none  [transposed_rows(): gathered = lax.all_gather(piece, 'prow', axis=2, tiled=True)]
    scatter x2 -> x0, local copies, waits for them, and re-layouts: 34.6 us -> none  [body(): state = changed.at[:, start_col:stop_col].set(panel_cols)]
    another operation x14 -> x2, other arithmetic: 32.6 us -> 0.02 us  [the longest x1 0.01 us: body(): jnp.stack([jnp.where(y >= 2, got[0], pack[0]), jnp.where(y // 2 != root /...]
    ppermute x0 -> x21, waiting for transfers between devices: none -> 28.3 us  [the longest x17 23.4 us: over_pcol(): return lax.ppermute(value, AXES, flat)]
    dot_general x4 -> x0, matrix products: 27.4 us -> none  [the longest x2 16.2 us: trailing_product(): lax.dot_general(rows_t, cols_t, (((0,), (0,)), ((), ())), precision=lax.P...]
    ppermute x0 -> x21, starting transfers between devices: none -> 26.4 us  [the longest x17 13.6 us: over_pcol(): return lax.ppermute(value, AXES, flat)]
  transfers between devices with their start and end apart: 4 -> 21, of which waited for: 4 -> 8; matrix products, arithmetic and copies ran while one was open for 1% -> 1% of each run, Pallas kernels for 0% -> 4%
where the time goes in v2:
time: 73.6 us; the launch traced here: 73.2 us
  waiting for transfers between devices  28.3 us (38%)
  starting transfers between devices  26.4 us (36%)
  Pallas kernels  15.9 us (22%)
  other arithmetic  1.17 us (2%)
  local copies, waits for them, and re-layouts  0.88 us (1%)
    ppermute x17, waiting for transfers between devices, over_pcol(): return lax.ppermute(value, AXES, flat)  23.4 us
    ppermute x17, starting transfers between devices, over_pcol(): return lax.ppermute(value, AXES, flat)  13.6 us
    ppermute x4, starting transfers between devices, over_prow(): return lax.ppermute(value, AXES, flat)  12.8 us
    pallas_call x1, Pallas kernels, body(): pl.pallas_call(finish_kernel, out_shape=jax.ShapeDtypeStruct((rows, cols)...  10.1 us
    pallas_call x2, Pallas kernels, body(): pl.pallas_call(functools.partial(pack_kernel, chips), out_shape=[jax.Shap...  5.75 us
    ppermute x4, waiting for transfers between devices, over_prow(): return lax.ppermute(value, AXES, flat)  4.97 us
  transfers between devices with their start and end apart: 21, of which 8 were waited for; matrix products, arithmetic and copies ran while one was open for 1% of the time, Pallas kernels for 4%

profile of v2, /device:TPU:1, one launch (start us, length us, event | category | flops | bytes accessed | tf_op | source)
XLA Modules:
  0.0 73.2 jit_solution(12087863454543854499)
XLA Ops:
  0.0 2.5 %pack.3 = (f32[896,128]{1,0:T(8,128)}, f32[896,128]{1,0:T(8,128)}, f32[896,128]{1,0:T(8,128)}) custom-call(f32[6144,256]{1,0:T(8,128)} %bitcast.35), custom_call_target="tpu_custom_call" | custom-call | tf_op jit(solution)/shard_map/pack/pallas_call | solution.py:191
  2.5 0.7 collective-permute-start.5
  3.2 0.7 collective-permute-start.6
  3.9 0.7 collective-permute-start
  4.6 3.3 %pack.2 = (f32[896,128]{1,0:T(8,128)}, f32[896,128]{1,0:T(8,128)}, f32[896,128]{1,0:T(8,128)}, f32[896,128]{1,0:T(8,128)}, f32[896,128]{1,0:T(8,128)}) custom-call(f32[6144,256]{1,0:T(8,128)} %bitcast.36), custom_call_target="tpu_custom_call" | custom-call | tf_op jit(solution)/shard_map/pack/pallas_call | solution.py:191
  7.9 0.7 collective-permute-start.1
  8.6 0.7 collective-permute-start.2
  9.3 0.0 collective-permute-done.5
  9.3 0.7 collective-permute-start.3
  10.0 0.0 collective-permute-done.6
  10.0 0.7 collective-permute-start.4
  10.7 0.8 %add.119 = f32[896,128]{1,0:T(8,128)} add(f32[896,128]{1,0:T(8,128)S(1)} %collective-permute-done.5, f32[896,128]{1,0:T(8,128)S(1)} %collective-permute-done.6) | non-fusion elementwise | flops 114688 | bytes 1376256 | tf_op jit(solution)/shard_map/add | solution.py:200
  11.5 0.0 collective-permute-done
  11.5 0.7 collective-permute-start.7
  12.2 0.0 collective-permute-done.1
  12.2 0.0 collective-permute-done.2
  12.2 0.0 collective-permute-done.3
  12.2 0.0 collective-permute-done.4
  12.2 0.0 collective-permute-done.7
  12.2 0.2 add_add_fusion
  12.4 1.3 %collective-permute-start.8 = (f32[896,128]{1,0:T(8,128)S(1)}, f32[896,128]{1,0:T(8,128)S(1)}, u32[]{:S(2)}, u32[]{:S(2)}) collective-permute-start(f32[896,128]{1,0:T(8,128)S(1)} %add_add_fusion), channel_id=1, source_target_pairs={{0,1},{2,3},{4,5},{6,7},{8,9},{10,11},{12,13},{14,15},{16,17},{18,... | collective-permute-start | bytes 1376264 | tf_op jit(solution)/shard_map/ppermute | solution.py:27
  13.7 17.5 %collective-permute-done.8 = f32[896,128]{1,0:T(8,128)S(1)} collective-permute-done((f32[896,128]{1,0:T(8,128)S(1)}, f32[896,128]{1,0:T(8,128)S(1)}, u32[]{:S(2)}, u32[]{:S(2)}) %collective-permute-start.8) | collective-permute-done | bytes 458784 | tf_op jit(solution)/shard_map/ppermute | solution.py:27
  31.3 0.1 add.121
  31.3 1.4 %collective-permute-start.9 = (f32[2,64,128]{2,1,0:T(8,128)S(1)}, f32[2,64,128]{2,1,0:T(8,128)S(1)}, u32[]{:S(2)}, u32[]{:S(2)}) collective-permute-start(f32[2,64,128]{2,1,0:T(8,128)S(1)} %bitcast.40), channel_id=1, source_target_pairs={{0,64},{16,80},{32,96},{48,112},{64,0},{80,16},{96,32},{112,48},{1... | collective-permute-start | bytes 196616 | tf_op jit(solution)/shard_map/ppermute | solution.py:32
  32.7 0.1 collective-permute-start.17
  32.8 0.1 collective-permute-start.15
  32.9 2.0 %collective-permute-done.9 = f32[2,64,128]{2,1,0:T(8,128)S(1)} collective-permute-done((f32[2,64,128]{2,1,0:T(8,128)S(1)}, f32[2,64,128]{2,1,0:T(8,128)S(1)}, u32[]{:S(2)}, u32[]{:S(2)}) %collective-permute-start.9) | collective-permute-done | bytes 65568 | tf_op jit(solution)/shard_map/ppermute | solution.py:32
  35.0 2.8 %collective-permute-start.10 = (f32[2,64,128]{2,1,0:T(8,128)S(1)}, f32[2,64,128]{2,1,0:T(8,128)S(1)}, u32[]{:S(2)}, u32[]{:S(2)}) collective-permute-start(f32[2,64,128]{2,1,0:T(8,128)S(1)} %pad_maximum_fusion.1), channel_id=1, source_target_pairs={{0,192},{16,208},{32,224},{48,240},{64,128},{80,144},{96,160},{112... | collective-permute-start | bytes 196616 | tf_op jit(solution)/shard_map/ppermute | solution.py:32
  37.8 0.7 collective-permute-start.13
  38.5 1.3 %collective-permute-done.10 = f32[2,64,128]{2,1,0:T(8,128)S(1)} collective-permute-done((f32[2,64,128]{2,1,0:T(8,128)S(1)}, f32[2,64,128]{2,1,0:T(8,128)S(1)}, u32[]{:S(2)}, u32[]{:S(2)}) %collective-permute-start.10) | collective-permute-done | bytes 65568 | tf_op jit(solution)/shard_map/ppermute | solution.py:32
  39.8 1.9 %collective-permute-done.17.refs_5_ = f32[768,128]{1,0:T(8,128)S(1)} collective-permute-done((f32[768,128]{1,0:T(8,128)S(1)}, f32[768,128]{1,0:T(8,128)S(1)}, u32[]{:S(2)}, u32[]{:S(2)}) %collective-permute-start.17) | collective-permute-done | bytes 393248 | tf_op jit(solution)/shard_map/ppermute | solution.py:27
  41.7 0.0 copy-start
  41.7 2.3 %collective-permute-done.15.refs_3_ = f32[768,128]{1,0:T(8,128)S(1)} collective-permute-done((f32[768,128]{1,0:T(8,128)S(1)}, f32[768,128]{1,0:T(8,128)S(1)}, u32[]{:S(2)}, u32[]{:S(2)}) %collective-permute-start.15) | collective-permute-done | bytes 393248 | tf_op jit(solution)/shard_map/ppermute | solution.py:27
  44.1 0.6 collective-permute-start.19
  44.7 3.1 %collective-permute-start.11 = (f32[2,64,128]{2,1,0:T(8,128)S(1)}, f32[2,64,128]{2,1,0:T(8,128)S(1)}, u32[]{:S(2)}, u32[]{:S(2)}) collective-permute-start(f32[2,64,128]{2,1,0:T(8,128)S(1)} %get-tuple-element.26), channel_id=1, source_target_pairs={{0,16},{16,0},{32,48},{48,32},{64,80},{80,64},{96,112},{112,96},{1... | collective-permute-start | bytes 196616 | tf_op jit(solution)/shard_map/ppermute | solution.py:32
  47.8 1.7 %collective-permute-done.11 = f32[2,64,128]{2,1,0:T(8,128)S(1)} collective-permute-done((f32[2,64,128]{2,1,0:T(8,128)S(1)}, f32[2,64,128]{2,1,0:T(8,128)S(1)}, u32[]{:S(2)}, u32[]{:S(2)}) %collective-permute-start.11) | collective-permute-done | bytes 65568 | tf_op jit(solution)/shard_map/ppermute | solution.py:32
  49.5 5.5 %collective-permute-start.12 = (f32[2,2,64,128]{3,2,1,0:T(8,128)S(1)}, f32[2,2,64,128]{3,2,1,0:T(8,128)S(1)}, u32[]{:S(2)}, u32[]{:S(2)}) collective-permute-start(f32[2,2,64,128]{3,2,1,0:T(8,128)S(1)} %copy.2), channel_id=1, source_target_pairs={{0,48},{16,32},{32,16},{48,0},{64,112},{80,96},{96,80},{112,64},{1... | collective-permute-start | bytes 393224 | tf_op jit(solution)/shard_map/ppermute | solution.py:32
  55.0 0.1 stack.71.info
  55.1 2.7 %collective-permute-start.18 = (f32[768,128]{1,0:T(8,128)S(1)}, f32[768,128]{1,0:T(8,128)S(1)}, u32[]{:S(2)}, u32[]{:S(2)}) collective-permute-start(f32[768,128]{1,0:T(8,128)S(1)} %collective-permute-done.17.refs_5_), channel_id=1, source_target_pairs={{0,1},{1,0},{2,3},{3,2},{4,5},{5,4},{6,7},{7,6},{8,9},{9,8},{10,11... | collective-permute-start | bytes 1179656 | tf_op jit(solution)/shard_map/ppermute | solution.py:27
  57.9 0.1 collective-permute-start.16
  58.0 0.0 collective-permute-done.13.refs_1_
  58.0 1.3 %collective-permute-start.14 = (f32[768,128]{1,0:T(8,128)S(1)}, f32[768,128]{1,0:T(8,128)S(1)}, u32[]{:S(2)}, u32[]{:S(2)}) collective-permute-start(f32[768,128]{1,0:T(8,128)S(1)} %collective-permute-done.13.refs_1_), channel_id=1, source_target_pairs={{0,1},{2,3},{4,5},{6,7},{8,9},{10,11},{12,13},{14,15},{16,17},{18,... | collective-permute-start | bytes 1179656 | tf_op jit(solution)/shard_map/ppermute | solution.py:27
  59.3 0.0 collective-permute-done.19.refs_7_
  59.3 0.0 copy-start.1
  59.3 1.2 %collective-permute-start.20 = (f32[768,128]{1,0:T(8,128)S(1)}, f32[768,128]{1,0:T(8,128)S(1)}, u32[]{:S(2)}, u32[]{:S(2)}) collective-permute-start(f32[768,128]{1,0:T(8,128)S(1)} %collective-permute-done.19.refs_7_), channel_id=1, source_target_pairs={{0,1},{1,0},{2,3},{3,2},{4,5},{5,4},{6,7},{7,6},{8,9},{9,8},{10,11... | collective-permute-start | bytes 1179656 | tf_op jit(solution)/shard_map/ppermute | solution.py:27
  60.5 0.0 collective-permute-done.12
  60.6 0.0 collective-permute-done.18.refs_6_
  60.6 0.0 copy-start.2
  60.6 0.0 collective-permute-done.16.refs_4_
  60.6 0.0 copy-start.3
  60.6 1.0 %collective-permute-done.14.refs_2_ = f32[768,128]{1,0:T(8,128)S(1)} collective-permute-done((f32[768,128]{1,0:T(8,128)S(1)}, f32[768,128]{1,0:T(8,128)S(1)}, u32[]{:S(2)}, u32[]{:S(2)}) %collective-permute-start.14) | collective-permute-done | bytes 393248 | tf_op jit(solution)/shard_map/ppermute | solution.py:27
  61.6 0.6 collective-permute-done.20.refs_8_
  62.1 0.0 copy-start.4
  62.1 0.0 copy-done
  62.1 0.0 copy-done.1
  62.1 0.0 copy-done.2
  62.1 0.0 copy-done.3
  62.2 0.7 %copy-done.4 = f32[768,128]{1,0:T(8,128)} copy-done((f32[768,128]{1,0:T(8,128)}, f32[768,128]{1,0:T(8,128)S(1)}, u32[]{:S(2)}) %copy-start.4) | copy-done | bytes 393240
  62.9 10.1 %finish.1 = f32[6144,256]{1,0:T(8,128)} custom-call(s32[11]{0:T(128)S(1)} %stack.71.info, f32[128,128]{1,0:T(8,128)S(1)} %bitcast.34, f32[256,128]{1,0:T(8,128)S(1)} %bitcast.33, f32[768,128]{1,0:T(8,128)S(1)} %slice.65.refs_0_, f32[768,128]{1,0:T(8,128)S(1)} %collective-permute-done.13.refs_1_, f32[768,128]{1,0:T(8,128)S(1)} %collective-permute-done.14.refs_2_, ...), custom_call_target="tpu_custom_call" | custom-call | tf_op jit(solution)/shard_map/finish/pallas_call | solution.py:255
  (12 shorter events, 0.2 us)
Async XLA Ops:
  2.5 6.8 %collective-permute-start.5 = (f32[896,128]{1,0:T(8,128)}, f32[896,128]{1,0:T(8,128)S(1)}, u32[]{:S(2)}, u32[]{:S(2)}) collective-permute-start(f32[896,128]{1,0:T(8,128)} %get-tuple-element.19), channel_id=1, source_target_pairs={{0,5},{16,21},{32,37},{48,53},{64,69},{80,85},{96,101},{112,117},{... | collective-permute-start | bytes 1376264 | tf_op jit(solution)/shard_map/ppermute | solution.py:27
  3.2 6.8 %collective-permute-start.6 = (f32[896,128]{1,0:T(8,128)}, f32[896,128]{1,0:T(8,128)S(1)}, u32[]{:S(2)}, u32[]{:S(2)}) collective-permute-start(f32[896,128]{1,0:T(8,128)} %get-tuple-element.20), channel_id=1, source_target_pairs={{0,13},{16,29},{32,45},{48,61},{64,77},{80,93},{96,109},{112,125},... | collective-permute-start | bytes 1376264 | tf_op jit(solution)/shard_map/ppermute | solution.py:27
  3.9 7.6 %collective-permute-start = (f32[896,128]{1,0:T(8,128)}, f32[896,128]{1,0:T(8,128)S(1)}, u32[]{:S(2)}, u32[]{:S(2)}) collective-permute-start(f32[896,128]{1,0:T(8,128)} %get-tuple-element.14), channel_id=1, source_target_pairs={{0,10},{16,26},{32,42},{48,58},{64,74},{80,90},{96,106},{112,122},... | collective-permute-start | bytes 1376264 | tf_op jit(solution)/shard_map/ppermute | solution.py:27
  7.9 4.3 %collective-permute-start.1 = (f32[896,128]{1,0:T(8,128)}, f32[896,128]{1,0:T(8,128)S(1)}, u32[]{:S(2)}, u32[]{:S(2)}) collective-permute-start(f32[896,128]{1,0:T(8,128)} %get-tuple-element.15), channel_id=1, source_target_pairs={{0,8},{16,24},{32,40},{48,56},{64,72},{80,88},{96,104},{112,120},{... | collective-permute-start | bytes 1376264 | tf_op jit(solution)/shard_map/ppermute | solution.py:27
  8.6 3.6 %collective-permute-start.2 = (f32[896,128]{1,0:T(8,128)}, f32[896,128]{1,0:T(8,128)S(1)}, u32[]{:S(2)}, u32[]{:S(2)}) collective-permute-start(f32[896,128]{1,0:T(8,128)} %get-tuple-element.16), channel_id=1, source_target_pairs={{0,12},{16,28},{32,44},{48,60},{64,76},{80,92},{96,108},{112,124},... | collective-permute-start | bytes 1376264 | tf_op jit(solution)/shard_map/ppermute | solution.py:27
  9.3 2.9 %collective-permute-start.3 = (f32[896,128]{1,0:T(8,128)}, f32[896,128]{1,0:T(8,128)S(1)}, u32[]{:S(2)}, u32[]{:S(2)}) collective-permute-start(f32[896,128]{1,0:T(8,128)} %get-tuple-element.17), channel_id=1, source_target_pairs={{0,2},{16,18},{32,34},{48,50},{64,66},{80,82},{96,98},{112,114},{1... | collective-permute-start | bytes 1376264 | tf_op jit(solution)/shard_map/ppermute | solution.py:27
  10.0 2.2 %collective-permute-start.4 = (f32[896,128]{1,0:T(8,128)}, f32[896,128]{1,0:T(8,128)S(1)}, u32[]{:S(2)}, u32[]{:S(2)}) collective-permute-start(f32[896,128]{1,0:T(8,128)} %get-tuple-element.18), channel_id=1, source_target_pairs={{0,4},{16,20},{32,36},{48,52},{64,68},{80,84},{96,100},{112,116},{... | collective-permute-start | bytes 1376264 | tf_op jit(solution)/shard_map/ppermute | solution.py:27
  11.5 0.7 %collective-permute-start.7 = (f32[896,128]{1,0:T(8,128)}, f32[896,128]{1,0:T(8,128)S(1)}, u32[]{:S(2)}, u32[]{:S(2)}) collective-permute-start(f32[896,128]{1,0:T(8,128)} %add.119), channel_id=1, source_target_pairs={{5,6},{13,14},{21,22},{29,30},{37,38},{45,46},{53,54},{61,62},{69,... | collective-permute-start | bytes 1376264 | tf_op jit(solution)/shard_map/ppermute | solution.py:27
  12.4 18.8 %collective-permute-start.8 = (f32[896,128]{1,0:T(8,128)S(1)}, f32[896,128]{1,0:T(8,128)S(1)}, u32[]{:S(2)}, u32[]{:S(2)}) collective-permute-start(f32[896,128]{1,0:T(8,128)S(1)} %add_add_fusion), channel_id=1, source_target_pairs={{0,1},{2,3},{4,5},{6,7},{8,9},{10,11},{12,13},{14,15},{16,17},{18,... | collective-permute-start | bytes 1376264 | tf_op jit(solution)/shard_map/ppermute | solution.py:27
  31.3 3.6 %collective-permute-start.9 = (f32[2,64,128]{2,1,0:T(8,128)S(1)}, f32[2,64,128]{2,1,0:T(8,128)S(1)}, u32[]{:S(2)}, u32[]{:S(2)}) collective-permute-start(f32[2,64,128]{2,1,0:T(8,128)S(1)} %bitcast.40), channel_id=1, source_target_pairs={{0,64},{16,80},{32,96},{48,112},{64,0},{80,16},{96,32},{112,48},{1... | collective-permute-start | bytes 196616 | tf_op jit(solution)/shard_map/ppermute | solution.py:32
  32.7 9.0 %collective-permute-start.17 = (f32[768,128]{1,0:T(8,128)S(1)}, f32[768,128]{1,0:T(8,128)S(1)}, u32[]{:S(2)}, u32[]{:S(2)}) collective-permute-start(f32[768,128]{1,0:T(8,128)S(1)} %slice.65.refs_0_), channel_id=1, source_target_pairs={{0,6},{2,4},{4,10},{6,8},{8,14},{10,12},{12,2},{14,0},{1,15},{3,13... | collective-permute-start | bytes 1179656 | tf_op jit(solution)/shard_map/ppermute | solution.py:27
  32.8 11.2 %collective-permute-start.15 = (f32[768,128]{1,0:T(8,128)S(1)}, f32[768,128]{1,0:T(8,128)S(1)}, u32[]{:S(2)}, u32[]{:S(2)}) collective-permute-start(f32[768,128]{1,0:T(8,128)S(1)} %slice.65.refs_0_), channel_id=1, source_target_pairs={{0,4},{2,6},{4,8},{6,10},{8,12},{10,14},{12,0},{14,2},{1,13},{3,15... | collective-permute-start | bytes 1179656 | tf_op jit(solution)/shard_map/ppermute | solution.py:27
  35.0 4.8 %collective-permute-start.10 = (f32[2,64,128]{2,1,0:T(8,128)S(1)}, f32[2,64,128]{2,1,0:T(8,128)S(1)}, u32[]{:S(2)}, u32[]{:S(2)}) collective-permute-start(f32[2,64,128]{2,1,0:T(8,128)S(1)} %pad_maximum_fusion.1), channel_id=1, source_target_pairs={{0,192},{16,208},{32,224},{48,240},{64,128},{80,144},{96,160},{112... | collective-permute-start | bytes 196616 | tf_op jit(solution)/shard_map/ppermute | solution.py:32
  37.8 20.1 %collective-permute-start.13 = (f32[768,128]{1,0:T(8,128)S(1)}, f32[768,128]{1,0:T(8,128)S(1)}, u32[]{:S(2)}, u32[]{:S(2)}) collective-permute-start(f32[768,128]{1,0:T(8,128)S(1)} %slice.65.refs_0_), channel_id=1, source_target_pairs={{0,2},{2,0},{4,6},{6,4},{8,10},{10,8},{12,14},{14,12},{16,18},{18,... | collective-permute-start | bytes 1179656 | tf_op jit(solution)/shard_map/ppermute | solution.py:27
  41.7 20.4 %copy-start = (f32[768,128]{1,0:T(8,128)}, f32[768,128]{1,0:T(8,128)S(1)}, u32[]{:S(2)}) copy-start(f32[768,128]{1,0:T(8,128)S(1)} %collective-permute-done.17.refs_5_) | copy-start | bytes 1179652
  44.1 15.2 %collective-permute-start.19 = (f32[768,128]{1,0:T(8,128)S(1)}, f32[768,128]{1,0:T(8,128)S(1)}, u32[]{:S(2)}, u32[]{:S(2)}) collective-permute-start(f32[768,128]{1,0:T(8,128)S(1)} %broadcast_select_fusion), channel_id=1, source_target_pairs={{0,4},{2,6},{4,8},{6,10},{8,12},{10,14},{12,0},{14,2},{1,13},{3,15... | collective-permute-start | bytes 1179656 | tf_op jit(solution)/shard_map/ppermute | solution.py:27
  44.7 4.7 %collective-permute-start.11 = (f32[2,64,128]{2,1,0:T(8,128)S(1)}, f32[2,64,128]{2,1,0:T(8,128)S(1)}, u32[]{:S(2)}, u32[]{:S(2)}) collective-permute-start(f32[2,64,128]{2,1,0:T(8,128)S(1)} %get-tuple-element.26), channel_id=1, source_target_pairs={{0,16},{16,0},{32,48},{48,32},{64,80},{80,64},{96,112},{112,96},{1... | collective-permute-start | bytes 196616 | tf_op jit(solution)/shard_map/ppermute | solution.py:32
  49.5 11.0 %collective-permute-start.12 = (f32[2,2,64,128]{3,2,1,0:T(8,128)S(1)}, f32[2,2,64,128]{3,2,1,0:T(8,128)S(1)}, u32[]{:S(2)}, u32[]{:S(2)}) collective-permute-start(f32[2,2,64,128]{3,2,1,0:T(8,128)S(1)} %copy.2), channel_id=1, source_target_pairs={{0,48},{16,32},{32,16},{48,0},{64,112},{80,96},{96,80},{112,64},{1... | collective-permute-start | bytes 393224 | tf_op jit(solution)/shard_map/ppermute | solution.py:32
  55.1 5.5 %collective-permute-start.18 = (f32[768,128]{1,0:T(8,128)S(1)}, f32[768,128]{1,0:T(8,128)S(1)}, u32[]{:S(2)}, u32[]{:S(2)}) collective-permute-start(f32[768,128]{1,0:T(8,128)S(1)} %collective-permute-done.17.refs_5_), channel_id=1, source_target_pairs={{0,1},{1,0},{2,3},{3,2},{4,5},{5,4},{6,7},{7,6},{8,9},{9,8},{10,11... | collective-permute-start | bytes 1179656 | tf_op jit(solution)/shard_map/ppermute | solution.py:27
  57.9 2.7 %collective-permute-start.16 = (f32[768,128]{1,0:T(8,128)S(1)}, f32[768,128]{1,0:T(8,128)S(1)}, u32[]{:S(2)}, u32[]{:S(2)}) collective-permute-start(f32[768,128]{1,0:T(8,128)S(1)} %collective-permute-done.15.refs_3_), channel_id=1, source_target_pairs={{0,1},{1,0},{2,3},{3,2},{4,5},{5,4},{6,7},{7,6},{8,9},{9,8},{10,11... | collective-permute-start | bytes 1179656 | tf_op jit(solution)/shard_map/ppermute | solution.py:27
  58.0 3.6 %collective-permute-start.14 = (f32[768,128]{1,0:T(8,128)S(1)}, f32[768,128]{1,0:T(8,128)S(1)}, u32[]{:S(2)}, u32[]{:S(2)}) collective-permute-start(f32[768,128]{1,0:T(8,128)S(1)} %collective-permute-done.13.refs_1_), channel_id=1, source_target_pairs={{0,1},{2,3},{4,5},{6,7},{8,9},{10,11},{12,13},{14,15},{16,17},{18,... | collective-permute-start | bytes 1179656 | tf_op jit(solution)/shard_map/ppermute | solution.py:27
  59.3 2.9 %copy-start.1 = (f32[768,128]{1,0:T(8,128)}, f32[768,128]{1,0:T(8,128)S(1)}, u32[]{:S(2)}) copy-start(f32[768,128]{1,0:T(8,128)S(1)} %collective-permute-done.19.refs_7_) | copy-start | bytes 1179652
  59.3 2.9 %collective-permute-start.20 = (f32[768,128]{1,0:T(8,128)S(1)}, f32[768,128]{1,0:T(8,128)S(1)}, u32[]{:S(2)}, u32[]{:S(2)}) collective-permute-start(f32[768,128]{1,0:T(8,128)S(1)} %collective-permute-done.19.refs_7_), channel_id=1, source_target_pairs={{0,1},{1,0},{2,3},{3,2},{4,5},{5,4},{6,7},{7,6},{8,9},{9,8},{10,11... | collective-permute-start | bytes 1179656 | tf_op jit(solution)/shard_map/ppermute | solution.py:27
  60.6 1.6 %copy-start.2 = (f32[768,128]{1,0:T(8,128)}, f32[768,128]{1,0:T(8,128)S(1)}, u32[]{:S(2)}) copy-start(f32[768,128]{1,0:T(8,128)S(1)} %collective-permute-done.18.refs_6_) | copy-start | bytes 1179652
  60.6 1.5 %copy-start.3 = (f32[768,128]{1,0:T(8,128)}, f32[768,128]{1,0:T(8,128)S(1)}, u32[]{:S(2)}) copy-start(f32[768,128]{1,0:T(8,128)S(1)} %collective-permute-done.16.refs_4_) | copy-start | bytes 1179652
  62.1 0.8 %copy-start.4 = (f32[768,128]{1,0:T(8,128)}, f32[768,128]{1,0:T(8,128)S(1)}, u32[]{:S(2)}) copy-start(f32[768,128]{1,0:T(8,128)S(1)} %collective-permute-done.20.refs_8_) | copy-start | bytes 1179652

commit v3 on v2

--- a/solution.py
+++ b/solution.py
@@ -49,50 +49,72 @@
             for j in range(8):
                 a = left[t][:, 8 * k + j : 8 * k + j + 1]
                 cols[t, j] = jnp.broadcast_to(a, (8, W2))
-        for s in range(8):
-            inv = lax.rsqrt(cols[k, s][s : s + 1])
-            lrow = left[k][s : s + 1] * inv
-            rrow = right[k][s : s + 1] * inv
-            up.append(lrow)
-            inv_rows.append(rrow)
-            pivots = {j: cols[k, j][s : s + 1] * inv for j in range(s + 1, 8)}
+        for s in range(0, 8, 2):
+            d0 = cols[k, s][s : s + 1]
+            e = cols[k, s][s + 1 : s + 2]
+            d1 = cols[k, s + 1][s + 1 : s + 2]
+            det = d0 * d1 - e * e
+            inv0 = lax.rsqrt(d0)
+            inv1 = lax.rsqrt(det) * (d0 * inv0)
+            lo0, ro0 = left[k][s : s + 1] * inv0, right[k][s : s + 1] * inv0
+            f10 = e * inv0
+            lo1 = (left[k][s + 1 : s + 2] - f10 * lo0) * inv1
+            ro1 = (right[k][s + 1 : s + 2] - f10 * ro0) * inv1
+            up += [lo0, lo1]
+            inv_rows += [ro0, ro1]
+            piv = {}
+            for j in range(s + 2, 8):
+                p0 = cols[k, j][s : s + 1] * inv0
+                piv[j] = (p0, (cols[k, j][s + 1 : s + 2] - f10 * p0) * inv1)
             for t in range(k, nt):
-                f = cols[t, s] * inv
+                f0 = cols[t, s] * inv0
+                f1 = (cols[t, s + 1] - f0 * f10) * inv1
                 if t == k:
-                    f = jnp.where(sub > s, f, 0.0)
-                for j in range(s + 1, 8):
-                    cols[t, j] = cols[t, j] - f * pivots[j]
-                left[t] = left[t] - f * lrow
-                right[t] = right[t] - f * rrow
+                    f0 = jnp.where(sub > s + 1, f0, 0.0)
+                    f1 = jnp.where(sub > s + 1, f1, 0.0)
+                for j in range(s + 2, 8):
+                    cols[t, j] = cols[t, j] - f0 * piv[j][0] - f1 * piv[j][1]
+                left[t] = left[t] - f0 * lo0 - f1 * lo1
+                right[t] = right[t] - f0 * ro0 - f1 * ro1
     upper = jnp.where(r <= c, jnp.concatenate(up, axis=0), 0.0)
     linv = jnp.where(r >= c, jnp.concatenate(inv_rows, axis=0), 0.0)
     return upper.T, linv, eye
 
 
-def pack_kernel(chips, local, *refs):
-    outs, sem = refs[:-1], refs[-1]
+def pack_kernel(chips, q_ref, local, *refs):
+    outs, (held, in_sem, out_sem) = refs[:-3], refs[-3:]
     part = outs[0].shape[0] - W2
-    copies = []
-    for k, g in enumerate(chips):
-        for j, (src, dst, n) in enumerate(
-            ((g * part, 0, part), (0, part, NB), (g // 2 * NB, part + NB, NB))
-        ):
-            copies.append(
-                pltpu.make_async_copy(
-                    local.at[pl.ds(src, n), pl.ds(0, W2)], outs[k].at[pl.ds(dst, n)], sem.at[k, j]
+
+    @pl.when(q_ref[0] == 0)
+    def _():
+        ins, copies = [], []
+        for k, g in enumerate(chips):
+            ins.append([])
+            for j, (src, dst, n) in enumerate(
+                ((g * part, 0, part), (0, part, NB), (g // 2 * NB, part + NB, NB))
+            ):
+                ins[k].append(
+                    pltpu.make_async_copy(
+                        local.at[pl.ds(src, n), pl.ds(0, W2)],
+                        held.at[k, pl.ds(dst, n)],
+                        in_sem.at[k, j],
+                    )
                 )
-            )
-    for copy in copies:
-        copy.start()
-    for copy in copies:
-        copy.wait()
+                ins[k][j].start()
+        for k in range(len(chips)):
+            for copy in ins[k]:
+                copy.wait()
+            copies.append(pltpu.make_async_copy(held.at[k], outs[k], out_sem.at[k]))
+            copies[k].start()
+        for copy in copies:
+            copy.wait()
 
 
 def finish_kernel(
     info, corner_ref, lead_ref, *refs
 ):
     bufs, state, out = refs[:9], refs[9], refs[10]
-    x_v, s_v, o_v, mhh, mlo, low_v, x_sem, s_sem, o_sem = refs[11:]
+    x_v, s_v, o_v, w_v, low_v, x_sem, s_sem, o_sem = refs[11:]
     rows, cols = s_v.shape[1:]
     core, p, q = info[8], info[9], info[10]
 
@@ -133,9 +155,9 @@
         linv, y, (((0,), (0,)), ((), ())), precision=HI, preferred_element_type=F32
     )
     hi = m.astype(BF16)
-    mhh[0:W2] = hi
-    mhh[W2 : 2 * W2] = hi
-    mlo[...] = (m - hi.astype(F32)).astype(BF16)
+    w_v[0:W2] = hi
+    w_v[W2 : 2 * W2] = hi
+    w_v[2 * W2 :] = (m - hi.astype(F32)).astype(BF16)
 
     def piece(k, carry):
         load_s(k).wait()
@@ -143,8 +165,7 @@
         x = x_v[k]
         xh = x.astype(BF16)
         xl = (x - xh.astype(F32)).astype(BF16)
-        prod = jnp.dot(jnp.concatenate([xh, xl], axis=1), mhh[...], preferred_element_type=F32)
-        prod += jnp.dot(xh, mlo[...], preferred_element_type=F32)
+        prod = jnp.dot(jnp.concatenate([xh, xl, xh], axis=1), w_v[...], preferred_element_type=F32)
         lane = lax.broadcasted_iota(jnp.int32, (1, cols), 1)
         replaced = (q == 0) & (lane < W2)
         o_v[k] = jnp.where(replaced, 0.0, s_v[k]) - prod
@@ -187,19 +208,23 @@
     hbm = pl.BlockSpec(memory_space=pl.ANY)
 
     messages = {}
-    for chips in ((3, 7, 5), (4, 6, 1, 2, 0)):
+    for chips in ((3, 7, 2, 4, 5, 1, 6, 0),):
         got = pl.pallas_call(
             functools.partial(pack_kernel, chips),
             out_shape=[jax.ShapeDtypeStruct((part + W2, W2), F32)] * len(chips),
-            in_specs=[hbm],
-            out_specs=[vmem] * len(chips),
-            scratch_shapes=[pltpu.SemaphoreType.DMA((len(chips), 3))],
+            in_specs=[smem, hbm],
+            out_specs=[hbm] * len(chips),
+            scratch_shapes=[
+                pltpu.VMEM((len(chips), part + W2, W2), F32),
+                pltpu.SemaphoreType.DMA((len(chips), 3)),
+                pltpu.SemaphoreType.DMA((len(chips),)),
+            ],
             name="pack",
-        )(local)
+        )(q.reshape(1).astype(jnp.int32), local)
         messages.update(zip(chips, got))
     relay = over_pcol(messages[3], [(0, 5)]) + over_pcol(messages[7], [(0, 13)])
     mine = jnp.where(is_src, messages[0], 0.0)
-    for g in (5, 4, 6, 1, 2):
+    for g in (2, 4, 5, 1, 6):
         mine = mine + over_pcol(messages[g], [(0, 2 * g)])
     mine = mine + over_pcol(relay, [(5, 6), (13, 14)])
     lend = [(2 * g, 2 * g + 1) for g in range(PIECES)]
@@ -261,8 +286,7 @@
             pltpu.VMEM((PIECES, part, W2), F32),
             pltpu.VMEM((PIECES, part, cols), F32),
             pltpu.VMEM((PIECES, part, cols), F32),
-            pltpu.VMEM((2 * W2, cols), BF16),
-            pltpu.VMEM((W2, cols), BF16),
+            pltpu.VMEM((3 * W2, cols), BF16),
             pltpu.VMEM((W2, W2), F32),
             pltpu.SemaphoreType.DMA((PIECES,)),
             pltpu.SemaphoreType.DMA((PIECES,)),

time: 73.6 us -> 69.9 us (0.950)
  Pallas kernels: 15.9 us -> 9.63 us
  waiting for transfers between devices: 28.3 us -> 34.2 us
  starting transfers between devices: 26.4 us -> 23.7 us
  other arithmetic: 1.17 us -> 0.39 us
    pallas_call x2 -> x1, Pallas kernels: 5.75 us -> 0.29 us  [body(): pl.pallas_call(functools.partial(pack_kernel, chips), out_shape=[jax.Shap...]
    ppermute x4, starting transfers between devices: 12.8 us -> 7.48 us  [over_prow(): return lax.ppermute(value, AXES, flat)]
    ppermute x17, waiting for transfers between devices: 23.4 us -> 26.5 us  [over_pcol(): return lax.ppermute(value, AXES, flat)]
    ppermute x4, waiting for transfers between devices: 4.97 us -> 7.63 us  [over_prow(): return lax.ppermute(value, AXES, flat)]
    ppermute x17, starting transfers between devices: 13.6 us -> 16.3 us  [over_pcol(): return lax.ppermute(value, AXES, flat)]
    pallas_call x1, Pallas kernels: 10.1 us -> 9.34 us  [body(): pl.pallas_call(finish_kernel, out_shape=jax.ShapeDtypeStruct((rows, cols)...]
    add x1, other arithmetic: 0.82 us -> 0.05 us  [body(): relay = over_pcol(messages[3], [(0, 5)]) + over_pcol(messages[7], [(0, 13)])]
  transfers between devices with their start and end apart: 21 -> 21, of which waited for: 8 -> 8; matrix products, arithmetic and copies ran while one was open for 1% -> 0% of each run, Pallas kernels for 4% -> 0%
where the time goes in v3:
time: 69.9 us; the launch traced here: 69.4 us
  waiting for transfers between devices  34.2 us (49%)
  starting transfers between devices  23.7 us (34%)
  Pallas kernels  9.63 us (14%)
  local copies, waits for them, and re-layouts  0.9 us (1%)
    ppermute x17, waiting for transfers between devices, over_pcol(): return lax.ppermute(value, AXES, flat)  26.5 us
    ppermute x17, starting transfers between devices, over_pcol(): return lax.ppermute(value, AXES, flat)  16.3 us
    pallas_call x1, Pallas kernels, body(): pl.pallas_call(finish_kernel, out_shape=jax.ShapeDtypeStruct((rows, cols)...  9.34 us
    ppermute x4, waiting for transfers between devices, over_prow(): return lax.ppermute(value, AXES, flat)  7.63 us
    ppermute x4, starting transfers between devices, over_prow(): return lax.ppermute(value, AXES, flat)  7.48 us
  transfers between devices with their start and end apart: 21, of which 8 were waited for; matrix products, arithmetic and copies ran while one was open for 0% of the time, Pallas kernels for 0%

profile of v3, /device:TPU:1, one launch (start us, length us, event | category | flops | bytes accessed | tf_op | source)
XLA Modules:
  0.0 69.4 jit_solution(15450641433019070790)
XLA Ops:
  0.0 0.3 pack.1
  0.3 0.7 collective-permute-start.5
  1.0 0.7 collective-permute-start.6
  1.7 0.7 collective-permute-start
  2.4 0.7 collective-permute-start.1
  3.1 0.7 collective-permute-start.2
  3.8 0.0 collective-permute-done.5
  3.8 0.7 collective-permute-start.3
  4.5 0.0 collective-permute-done.6
  4.5 0.7 collective-permute-start.4
  5.2 0.1 add.119
  5.3 0.0 collective-permute-done
  5.3 0.7 collective-permute-start.7
  6.0 0.0 collective-permute-done.1
  6.0 0.0 collective-permute-done.2
  6.0 0.0 collective-permute-done.3
  6.0 0.0 collective-permute-done.4
  6.0 0.0 collective-permute-done.7
  6.0 0.2 add_add_fusion
  6.2 1.3 %collective-permute-start.8 = (f32[896,128]{1,0:T(8,128)S(1)}, f32[896,128]{1,0:T(8,128)S(1)}, u32[]{:S(2)}, u32[]{:S(2)}) collective-permute-start(f32[896,128]{1,0:T(8,128)S(1)} %add_add_fusion), channel_id=1, source_target_pairs={{0,1},{2,3},{4,5},{6,7},{8,9},{10,11},{12,13},{14,15},{16,17},{18,... | collective-permute-start | bytes 1376264 | tf_op jit(solution)/shard_map/ppermute | solution.py:27
  7.5 20.8 %collective-permute-done.8 = f32[896,128]{1,0:T(8,128)S(1)} collective-permute-done((f32[896,128]{1,0:T(8,128)S(1)}, f32[896,128]{1,0:T(8,128)S(1)}, u32[]{:S(2)}, u32[]{:S(2)}) %collective-permute-start.8) | collective-permute-done | bytes 458784 | tf_op jit(solution)/shard_map/ppermute | solution.py:27
  28.3 0.1 add.121
  28.4 0.1 collective-permute-start.9
  28.6 2.5 %collective-permute-start.17 = (f32[768,128]{1,0:T(8,128)S(1)}, f32[768,128]{1,0:T(8,128)S(1)}, u32[]{:S(2)}, u32[]{:S(2)}) collective-permute-start(f32[768,128]{1,0:T(8,128)S(1)} %slice.65.refs_0_), channel_id=1, source_target_pairs={{0,6},{2,4},{4,10},{6,8},{8,14},{10,12},{12,2},{14,0},{1,15},{3,13... | collective-permute-start | bytes 1179656 | tf_op jit(solution)/shard_map/ppermute | solution.py:27
  31.1 0.0 collective-permute-start.15
  31.1 0.9 %collective-permute-done.9 = f32[2,64,128]{2,1,0:T(8,128)S(1)} collective-permute-done((f32[2,64,128]{2,1,0:T(8,128)S(1)}, f32[2,64,128]{2,1,0:T(8,128)S(1)}, u32[]{:S(2)}, u32[]{:S(2)}) %collective-permute-start.9) | collective-permute-done | bytes 65568 | tf_op jit(solution)/shard_map/ppermute | solution.py:32
  32.1 1.1 %collective-permute-start.10 = (f32[2,64,128]{2,1,0:T(8,128)S(1)}, f32[2,64,128]{2,1,0:T(8,128)S(1)}, u32[]{:S(2)}, u32[]{:S(2)}) collective-permute-start(f32[2,64,128]{2,1,0:T(8,128)S(1)} %pad_maximum_fusion.1), channel_id=1, source_target_pairs={{0,192},{16,208},{32,224},{48,240},{64,128},{80,144},{96,160},{112... | collective-permute-start | bytes 196616 | tf_op jit(solution)/shard_map/ppermute | solution.py:32
  33.1 0.7 collective-permute-start.13
  33.8 2.9 %collective-permute-done.10 = f32[2,64,128]{2,1,0:T(8,128)S(1)} collective-permute-done((f32[2,64,128]{2,1,0:T(8,128)S(1)}, f32[2,64,128]{2,1,0:T(8,128)S(1)}, u32[]{:S(2)}, u32[]{:S(2)}) %collective-permute-start.10) | collective-permute-done | bytes 65568 | tf_op jit(solution)/shard_map/ppermute | solution.py:32
  36.8 2.9 %collective-permute-done.17.refs_5_ = f32[768,128]{1,0:T(8,128)S(1)} collective-permute-done((f32[768,128]{1,0:T(8,128)S(1)}, f32[768,128]{1,0:T(8,128)S(1)}, u32[]{:S(2)}, u32[]{:S(2)}) %collective-permute-start.17) | collective-permute-done | bytes 393248 | tf_op jit(solution)/shard_map/ppermute | solution.py:27
  39.6 0.0 copy-start
  39.6 1.3 %collective-permute-done.15.refs_3_ = f32[768,128]{1,0:T(8,128)S(1)} collective-permute-done((f32[768,128]{1,0:T(8,128)S(1)}, f32[768,128]{1,0:T(8,128)S(1)}, u32[]{:S(2)}, u32[]{:S(2)}) %collective-permute-start.15) | collective-permute-done | bytes 393248 | tf_op jit(solution)/shard_map/ppermute | solution.py:27
  41.0 2.2 %collective-permute-start.19 = (f32[768,128]{1,0:T(8,128)S(1)}, f32[768,128]{1,0:T(8,128)S(1)}, u32[]{:S(2)}, u32[]{:S(2)}) collective-permute-start(f32[768,128]{1,0:T(8,128)S(1)} %broadcast_select_fusion), channel_id=1, source_target_pairs={{0,4},{2,6},{4,8},{6,10},{8,12},{10,14},{12,0},{14,2},{1,13},{3,15... | collective-permute-start | bytes 1179656 | tf_op jit(solution)/shard_map/ppermute | solution.py:27
  43.2 2.6 %collective-permute-start.11 = (f32[2,64,128]{2,1,0:T(8,128)S(1)}, f32[2,64,128]{2,1,0:T(8,128)S(1)}, u32[]{:S(2)}, u32[]{:S(2)}) collective-permute-start(f32[2,64,128]{2,1,0:T(8,128)S(1)} %get-tuple-element.26), channel_id=1, source_target_pairs={{0,16},{16,0},{32,48},{48,32},{64,80},{80,64},{96,112},{112,96},{1... | collective-permute-start | bytes 196616 | tf_op jit(solution)/shard_map/ppermute | solution.py:32
  45.7 3.8 %collective-permute-done.11 = f32[2,64,128]{2,1,0:T(8,128)S(1)} collective-permute-done((f32[2,64,128]{2,1,0:T(8,128)S(1)}, f32[2,64,128]{2,1,0:T(8,128)S(1)}, u32[]{:S(2)}, u32[]{:S(2)}) %collective-permute-start.11) | collective-permute-done | bytes 65568 | tf_op jit(solution)/shard_map/ppermute | solution.py:32
  49.5 3.7 %collective-permute-start.12 = (f32[2,2,64,128]{3,2,1,0:T(8,128)S(1)}, f32[2,2,64,128]{3,2,1,0:T(8,128)S(1)}, u32[]{:S(2)}, u32[]{:S(2)}) collective-permute-start(f32[2,2,64,128]{3,2,1,0:T(8,128)S(1)} %copy.2), channel_id=1, source_target_pairs={{0,48},{16,32},{32,16},{48,0},{64,112},{80,96},{96,80},{112,64},{1... | collective-permute-start | bytes 393224 | tf_op jit(solution)/shard_map/ppermute | solution.py:32
  53.3 0.1 stack.71.info
  53.4 1.5 %collective-permute-start.18 = (f32[768,128]{1,0:T(8,128)S(1)}, f32[768,128]{1,0:T(8,128)S(1)}, u32[]{:S(2)}, u32[]{:S(2)}) collective-permute-start(f32[768,128]{1,0:T(8,128)S(1)} %collective-permute-done.17.refs_5_), channel_id=1, source_target_pairs={{0,1},{1,0},{2,3},{3,2},{4,5},{5,4},{6,7},{7,6},{8,9},{9,8},{10,11... | collective-permute-start | bytes 1179656 | tf_op jit(solution)/shard_map/ppermute | solution.py:27
  54.8 0.1 collective-permute-start.16
  54.9 0.0 collective-permute-done.13.refs_1_
  54.9 1.3 %collective-permute-start.14 = (f32[768,128]{1,0:T(8,128)S(1)}, f32[768,128]{1,0:T(8,128)S(1)}, u32[]{:S(2)}, u32[]{:S(2)}) collective-permute-start(f32[768,128]{1,0:T(8,128)S(1)} %collective-permute-done.13.refs_1_), channel_id=1, source_target_pairs={{0,1},{2,3},{4,5},{6,7},{8,9},{10,11},{12,13},{14,15},{16,17},{18,... | collective-permute-start | bytes 1179656 | tf_op jit(solution)/shard_map/ppermute | solution.py:27
  56.2 0.0 collective-permute-done.19.refs_7_
  56.2 0.0 copy-start.1
  56.2 1.2 %collective-permute-start.20 = (f32[768,128]{1,0:T(8,128)S(1)}, f32[768,128]{1,0:T(8,128)S(1)}, u32[]{:S(2)}, u32[]{:S(2)}) collective-permute-start(f32[768,128]{1,0:T(8,128)S(1)} %collective-permute-done.19.refs_7_), channel_id=1, source_target_pairs={{0,1},{1,0},{2,3},{3,2},{4,5},{5,4},{6,7},{7,6},{8,9},{9,8},{10,11... | collective-permute-start | bytes 1179656 | tf_op jit(solution)/shard_map/ppermute | solution.py:27
  57.5 0.0 collective-permute-done.12
  57.5 0.0 collective-permute-done.18.refs_6_
  57.5 0.0 copy-start.2
  57.5 0.0 collective-permute-done.16.refs_4_
  57.5 0.0 copy-start.3
  57.6 1.0 %collective-permute-done.14.refs_2_ = f32[768,128]{1,0:T(8,128)S(1)} collective-permute-done((f32[768,128]{1,0:T(8,128)S(1)}, f32[768,128]{1,0:T(8,128)S(1)}, u32[]{:S(2)}, u32[]{:S(2)}) %collective-permute-start.14) | collective-permute-done | bytes 393248 | tf_op jit(solution)/shard_map/ppermute | solution.py:27
  58.5 0.6 collective-permute-done.20.refs_8_
  59.1 0.0 copy-start.4
  59.1 0.0 copy-done
  59.1 0.0 copy-done.1
  59.1 0.0 copy-done.2
  59.1 0.0 copy-done.3
  59.1 0.8 %copy-done.4 = f32[768,128]{1,0:T(8,128)} copy-done((f32[768,128]{1,0:T(8,128)}, f32[768,128]{1,0:T(8,128)S(1)}, u32[]{:S(2)}) %copy-start.4) | copy-done | bytes 393240
  59.9 9.3 %finish.1 = f32[6144,256]{1,0:T(8,128)} custom-call(s32[11]{0:T(128)S(1)} %stack.71.info, f32[128,128]{1,0:T(8,128)S(1)} %bitcast.34, f32[256,128]{1,0:T(8,128)S(1)} %bitcast.33, f32[768,128]{1,0:T(8,128)S(1)} %slice.65.refs_0_, f32[768,128]{1,0:T(8,128)S(1)} %collective-permute-done.13.refs_1_, f32[768,128]{1,0:T(8,128)S(1)} %collective-permute-done.14.refs_2_, ...), custom_call_target="tpu_custom_call" | custom-call | tf_op jit(solution)/shard_map/finish/pallas_call | solution.py:280
  (12 shorter events, 0.2 us)
Async XLA Ops:
  0.3 3.5 %collective-permute-start.5 = (f32[896,128]{1,0:T(8,128)}, f32[896,128]{1,0:T(8,128)S(1)}, u32[]{:S(2)}, u32[]{:S(2)}) collective-permute-start(f32[896,128]{1,0:T(8,128)} %get-tuple-element.19), channel_id=1, source_target_pairs={{0,5},{16,21},{32,37},{48,53},{64,69},{80,85},{96,101},{112,117},{... | collective-permute-start | bytes 1376264 | tf_op jit(solution)/shard_map/ppermute | solution.py:27
  1.0 3.5 %collective-permute-start.6 = (f32[896,128]{1,0:T(8,128)}, f32[896,128]{1,0:T(8,128)S(1)}, u32[]{:S(2)}, u32[]{:S(2)}) collective-permute-start(f32[896,128]{1,0:T(8,128)} %get-tuple-element.20), channel_id=1, source_target_pairs={{0,13},{16,29},{32,45},{48,61},{64,77},{80,93},{96,109},{112,125},... | collective-permute-start | bytes 1376264 | tf_op jit(solution)/shard_map/ppermute | solution.py:27
  1.7 3.6 %collective-permute-start = (f32[896,128]{1,0:T(8,128)}, f32[896,128]{1,0:T(8,128)S(1)}, u32[]{:S(2)}, u32[]{:S(2)}) collective-permute-start(f32[896,128]{1,0:T(8,128)} %get-tuple-element.14), channel_id=1, source_target_pairs={{0,4},{16,20},{32,36},{48,52},{64,68},{80,84},{96,100},{112,116},{... | collective-permute-start | bytes 1376264 | tf_op jit(solution)/shard_map/ppermute | solution.py:27
  2.4 3.6 %collective-permute-start.1 = (f32[896,128]{1,0:T(8,128)}, f32[896,128]{1,0:T(8,128)S(1)}, u32[]{:S(2)}, u32[]{:S(2)}) collective-permute-start(f32[896,128]{1,0:T(8,128)} %get-tuple-element.15), channel_id=1, source_target_pairs={{0,8},{16,24},{32,40},{48,56},{64,72},{80,88},{96,104},{112,120},{... | collective-permute-start | bytes 1376264 | tf_op jit(solution)/shard_map/ppermute | solution.py:27
  3.1 2.9 %collective-permute-start.2 = (f32[896,128]{1,0:T(8,128)}, f32[896,128]{1,0:T(8,128)S(1)}, u32[]{:S(2)}, u32[]{:S(2)}) collective-permute-start(f32[896,128]{1,0:T(8,128)} %get-tuple-element.16), channel_id=1, source_target_pairs={{0,10},{16,26},{32,42},{48,58},{64,74},{80,90},{96,106},{112,122},... | collective-permute-start | bytes 1376264 | tf_op jit(solution)/shard_map/ppermute | solution.py:27
  3.8 2.2 %collective-permute-start.3 = (f32[896,128]{1,0:T(8,128)}, f32[896,128]{1,0:T(8,128)S(1)}, u32[]{:S(2)}, u32[]{:S(2)}) collective-permute-start(f32[896,128]{1,0:T(8,128)} %get-tuple-element.17), channel_id=1, source_target_pairs={{0,2},{16,18},{32,34},{48,50},{64,66},{80,82},{96,98},{112,114},{1... | collective-permute-start | bytes 1376264 | tf_op jit(solution)/shard_map/ppermute | solution.py:27
  4.5 1.5 %collective-permute-start.4 = (f32[896,128]{1,0:T(8,128)}, f32[896,128]{1,0:T(8,128)S(1)}, u32[]{:S(2)}, u32[]{:S(2)}) collective-permute-start(f32[896,128]{1,0:T(8,128)} %get-tuple-element.18), channel_id=1, source_target_pairs={{0,12},{16,28},{32,44},{48,60},{64,76},{80,92},{96,108},{112,124},... | collective-permute-start | bytes 1376264 | tf_op jit(solution)/shard_map/ppermute | solution.py:27
  5.3 0.7 %collective-permute-start.7 = (f32[896,128]{1,0:T(8,128)S(1)}, f32[896,128]{1,0:T(8,128)S(1)}, u32[]{:S(2)}, u32[]{:S(2)}) collective-permute-start(f32[896,128]{1,0:T(8,128)S(1)} %add.119), channel_id=1, source_target_pairs={{5,6},{13,14},{21,22},{29,30},{37,38},{45,46},{53,54},{61,62},{69,... | collective-permute-start | bytes 1376264 | tf_op jit(solution)/shard_map/ppermute | solution.py:27
  6.2 22.1 %collective-permute-start.8 = (f32[896,128]{1,0:T(8,128)S(1)}, f32[896,128]{1,0:T(8,128)S(1)}, u32[]{:S(2)}, u32[]{:S(2)}) collective-permute-start(f32[896,128]{1,0:T(8,128)S(1)} %add_add_fusion), channel_id=1, source_target_pairs={{0,1},{2,3},{4,5},{6,7},{8,9},{10,11},{12,13},{14,15},{16,17},{18,... | collective-permute-start | bytes 1376264 | tf_op jit(solution)/shard_map/ppermute | solution.py:27
  28.4 3.6 %collective-permute-start.9 = (f32[2,64,128]{2,1,0:T(8,128)S(1)}, f32[2,64,128]{2,1,0:T(8,128)S(1)}, u32[]{:S(2)}, u32[]{:S(2)}) collective-permute-start(f32[2,64,128]{2,1,0:T(8,128)S(1)} %bitcast.39), channel_id=1, source_target_pairs={{0,64},{16,80},{32,96},{48,112},{64,0},{80,16},{96,32},{112,48},{1... | collective-permute-start | bytes 196616 | tf_op jit(solution)/shard_map/ppermute | solution.py:32
  28.6 11.1 %collective-permute-start.17 = (f32[768,128]{1,0:T(8,128)S(1)}, f32[768,128]{1,0:T(8,128)S(1)}, u32[]{:S(2)}, u32[]{:S(2)}) collective-permute-start(f32[768,128]{1,0:T(8,128)S(1)} %slice.65.refs_0_), channel_id=1, source_target_pairs={{0,6},{2,4},{4,10},{6,8},{8,14},{10,12},{12,2},{14,0},{1,15},{3,13... | collective-permute-start | bytes 1179656 | tf_op jit(solution)/shard_map/ppermute | solution.py:27
  31.1 9.8 %collective-permute-start.15 = (f32[768,128]{1,0:T(8,128)S(1)}, f32[768,128]{1,0:T(8,128)S(1)}, u32[]{:S(2)}, u32[]{:S(2)}) collective-permute-start(f32[768,128]{1,0:T(8,128)S(1)} %slice.65.refs_0_), channel_id=1, source_target_pairs={{0,4},{2,6},{4,8},{6,10},{8,12},{10,14},{12,0},{14,2},{1,13},{3,15... | collective-permute-start | bytes 1179656 | tf_op jit(solution)/shard_map/ppermute | solution.py:27
  32.1 4.7 %collective-permute-start.10 = (f32[2,64,128]{2,1,0:T(8,128)S(1)}, f32[2,64,128]{2,1,0:T(8,128)S(1)}, u32[]{:S(2)}, u32[]{:S(2)}) collective-permute-start(f32[2,64,128]{2,1,0:T(8,128)S(1)} %pad_maximum_fusion.1), channel_id=1, source_target_pairs={{0,192},{16,208},{32,224},{48,240},{64,128},{80,144},{96,160},{112... | collective-permute-start | bytes 196616 | tf_op jit(solution)/shard_map/ppermute | solution.py:32
  33.1 21.8 %collective-permute-start.13 = (f32[768,128]{1,0:T(8,128)S(1)}, f32[768,128]{1,0:T(8,128)S(1)}, u32[]{:S(2)}, u32[]{:S(2)}) collective-permute-start(f32[768,128]{1,0:T(8,128)S(1)} %slice.65.refs_0_), channel_id=1, source_target_pairs={{0,2},{2,0},{4,6},{6,4},{8,10},{10,8},{12,14},{14,12},{16,18},{18,... | collective-permute-start | bytes 1179656 | tf_op jit(solution)/shard_map/ppermute | solution.py:27
  39.6 19.5 %copy-start = (f32[768,128]{1,0:T(8,128)}, f32[768,128]{1,0:T(8,128)S(1)}, u32[]{:S(2)}) copy-start(f32[768,128]{1,0:T(8,128)S(1)} %collective-permute-done.17.refs_5_) | copy-start | bytes 1179652
  41.0 15.2 %collective-permute-start.19 = (f32[768,128]{1,0:T(8,128)S(1)}, f32[768,128]{1,0:T(8,128)S(1)}, u32[]{:S(2)}, u32[]{:S(2)}) collective-permute-start(f32[768,128]{1,0:T(8,128)S(1)} %broadcast_select_fusion), channel_id=1, source_target_pairs={{0,4},{2,6},{4,8},{6,10},{8,12},{10,14},{12,0},{14,2},{1,13},{3,15... | collective-permute-start | bytes 1179656 | tf_op jit(solution)/shard_map/ppermute | solution.py:27
  43.2 6.3 %collective-permute-start.11 = (f32[2,64,128]{2,1,0:T(8,128)S(1)}, f32[2,64,128]{2,1,0:T(8,128)S(1)}, u32[]{:S(2)}, u32[]{:S(2)}) collective-permute-start(f32[2,64,128]{2,1,0:T(8,128)S(1)} %get-tuple-element.26), channel_id=1, source_target_pairs={{0,16},{16,0},{32,48},{48,32},{64,80},{80,64},{96,112},{112,96},{1... | collective-permute-start | bytes 196616 | tf_op jit(solution)/shard_map/ppermute | solution.py:32
  49.5 7.9 %collective-permute-start.12 = (f32[2,2,64,128]{3,2,1,0:T(8,128)S(1)}, f32[2,2,64,128]{3,2,1,0:T(8,128)S(1)}, u32[]{:S(2)}, u32[]{:S(2)}) collective-permute-start(f32[2,2,64,128]{3,2,1,0:T(8,128)S(1)} %copy.2), channel_id=1, source_target_pairs={{0,48},{16,32},{32,16},{48,0},{64,112},{80,96},{96,80},{112,64},{1... | collective-permute-start | bytes 393224 | tf_op jit(solution)/shard_map/ppermute | solution.py:32
  53.4 4.2 %collective-permute-start.18 = (f32[768,128]{1,0:T(8,128)S(1)}, f32[768,128]{1,0:T(8,128)S(1)}, u32[]{:S(2)}, u32[]{:S(2)}) collective-permute-start(f32[768,128]{1,0:T(8,128)S(1)} %collective-permute-done.17.refs_5_), channel_id=1, source_target_pairs={{0,1},{1,0},{2,3},{3,2},{4,5},{5,4},{6,7},{7,6},{8,9},{9,8},{10,11... | collective-permute-start | bytes 1179656 | tf_op jit(solution)/shard_map/ppermute | solution.py:27
  54.8 2.7 %collective-permute-start.16 = (f32[768,128]{1,0:T(8,128)S(1)}, f32[768,128]{1,0:T(8,128)S(1)}, u32[]{:S(2)}, u32[]{:S(2)}) collective-permute-start(f32[768,128]{1,0:T(8,128)S(1)} %collective-permute-done.15.refs_3_), channel_id=1, source_target_pairs={{0,1},{1,0},{2,3},{3,2},{4,5},{5,4},{6,7},{7,6},{8,9},{9,8},{10,11... | collective-permute-start | bytes 1179656 | tf_op jit(solution)/shard_map/ppermute | solution.py:27
  54.9 3.6 %collective-permute-start.14 = (f32[768,128]{1,0:T(8,128)S(1)}, f32[768,128]{1,0:T(8,128)S(1)}, u32[]{:S(2)}, u32[]{:S(2)}) collective-permute-start(f32[768,128]{1,0:T(8,128)S(1)} %collective-permute-done.13.refs_1_), channel_id=1, source_target_pairs={{0,1},{2,3},{4,5},{6,7},{8,9},{10,11},{12,13},{14,15},{16,17},{18,... | collective-permute-start | bytes 1179656 | tf_op jit(solution)/shard_map/ppermute | solution.py:27
  56.2 2.9 %copy-start.1 = (f32[768,128]{1,0:T(8,128)}, f32[768,128]{1,0:T(8,128)S(1)}, u32[]{:S(2)}) copy-start(f32[768,128]{1,0:T(8,128)S(1)} %collective-permute-done.19.refs_7_) | copy-start | bytes 1179652
  56.2 2.9 %collective-permute-start.20 = (f32[768,128]{1,0:T(8,128)S(1)}, f32[768,128]{1,0:T(8,128)S(1)}, u32[]{:S(2)}, u32[]{:S(2)}) collective-permute-start(f32[768,128]{1,0:T(8,128)S(1)} %collective-permute-done.19.refs_7_), channel_id=1, source_target_pairs={{0,1},{1,0},{2,3},{3,2},{4,5},{5,4},{6,7},{7,6},{8,9},{9,8},{10,11... | collective-permute-start | bytes 1179656 | tf_op jit(solution)/shard_map/ppermute | solution.py:27
  57.5 1.6 %copy-start.2 = (f32[768,128]{1,0:T(8,128)}, f32[768,128]{1,0:T(8,128)S(1)}, u32[]{:S(2)}) copy-start(f32[768,128]{1,0:T(8,128)S(1)} %collective-permute-done.18.refs_6_) | copy-start | bytes 1179652
  57.5 1.5 %copy-start.3 = (f32[768,128]{1,0:T(8,128)}, f32[768,128]{1,0:T(8,128)S(1)}, u32[]{:S(2)}) copy-start(f32[768,128]{1,0:T(8,128)S(1)} %collective-permute-done.16.refs_4_) | copy-start | bytes 1179652
  59.1 0.8 %copy-start.4 = (f32[768,128]{1,0:T(8,128)}, f32[768,128]{1,0:T(8,128)S(1)}, u32[]{:S(2)}) copy-start(f32[768,128]{1,0:T(8,128)S(1)} %collective-permute-done.20.refs_8_) | copy-start | bytes 1179652

commit v4 on v3

--- a/solution.py
+++ b/solution.py
@@ -233,22 +233,15 @@
     pack = mine[part:].reshape(2, NB, W2)
 
     root = q % 4
-    got = over_prow(pack, [(s, s ^ 4) for s in range(NP)])
-    pack = jnp.stack([jnp.where(y == 1, got[0], pack[0]), jnp.where(y == root ^ 1, got[1], pack[1])])
-    got = over_prow(pack, [(s, s ^ 12) for s in range(NP)])
-    pack = jnp.stack(
-        [jnp.where(y >= 2, got[0], pack[0]), jnp.where(y // 2 != root // 2, got[1], pack[1])]
-    )
-    got = over_prow(pack, [(s, s ^ 1) for s in range(NP)])
-    odd = z % 2 == 1
-    pack = jnp.where(odd, jnp.stack([got, pack], 1), jnp.stack([pack, got], 1))
     got = over_prow(pack, [(s, s ^ 3) for s in range(NP)])
     high = z >= 2
-    corner = jnp.where(high, got[0], pack[0]).reshape(W2, W2)
-    lead = jnp.concatenate(
-        [jnp.where(high, got, pack)[1], jnp.where(high, pack, got)[1]]
-    ).reshape(4 * NB, W2)
-
+    pack = jnp.stack(
+        [
+            jnp.where(high, got[0], pack[0]),
+            jnp.where(high, got[1], pack[1]),
+            jnp.where(high, pack[1], got[1]),
+        ]
+    )
     swap = [(s, s ^ 1) for s in range(NQ)]
 
     def send(value, m0, m1):
@@ -265,15 +258,24 @@
     later = both
     cross = send(later, (1, 1), (-1, 1))
     over = send(later, (0, 1), None)
+    got = over_prow(pack, [(s, s ^ 4) for s in range(NP)])
+    is_corner = jnp.arange(3)[:, None, None] == 0
+    pack = jnp.where(jnp.where(is_corner, y == 1, y == root ^ 1), got, pack)
+    got = over_prow(pack, [(s, s ^ 12) for s in range(NP)])
+    pack = jnp.where(jnp.where(is_corner, y >= 2, y // 2 != root // 2), got, pack)
+    sides = lax.optimization_barrier((pack, side, cross, over))
+    got = over_prow(sides[0], [(s, s ^ 1) for s in range(NP)])
     again = send(jnp.where(core == 0, side, cross), (1, 0), (-1, 0))
-    bufs = [both, over, over_pcol(over, lend)]
+    lent = over_pcol(sides[3], lend)
+    side_s, cross_s, again_s = (over_pcol(value, swap) for value in (sides[1], sides[2], again))
+    outer = (z == 0) | (z == 3)
+    first, second = jnp.where(outer, pack, got), jnp.where(outer, got, pack)
+    corner = jnp.concatenate([first[0], second[0]])
+    lead = jnp.concatenate([first[1], second[1], second[2], first[2]])
+
+    bufs = [both, over, lent, side, side_s, cross, cross_s, again, again_s]
     owners = [chip, chip // 2 * 2 + 1 - chip % 2]
-    for got, moves in (
-        (side, ((1, 0), (-1, 0))),
-        (cross, ((1, 1), (-1, 1))),
-        (again, ((2, 0), (-2, 1))),
-    ):
-        bufs += [got, over_pcol(got, swap)]
+    for moves in (((1, 0), (-1, 0)), ((1, 1), (-1, 1)), ((2, 0), (-2, 1))):
         owners += owner(*moves)
 
     info = jnp.stack([o.astype(jnp.int32) for o in owners + [core, p, q]])

time: 69.9 us -> 68.5 us (0.980)
  waiting for transfers between devices: 34.2 us -> 26.7 us
  starting transfers between devices: 23.7 us -> 29.8 us
    ppermute x4, waiting for transfers between devices: 7.63 us -> 1.79 us  [over_prow(): return lax.ppermute(value, AXES, flat)]
    ppermute x17, starting transfers between devices: 16.3 us -> 19.6 us  [over_pcol(): return lax.ppermute(value, AXES, flat)]
    ppermute x4, starting transfers between devices: 7.48 us -> 10.2 us  [over_prow(): return lax.ppermute(value, AXES, flat)]
    ppermute x17, waiting for transfers between devices: 26.5 us -> 24.9 us  [over_pcol(): return lax.ppermute(value, AXES, flat)]
  transfers between devices with their start and end apart: 21 -> 21, of which waited for: 8 -> 5; matrix products, arithmetic and copies ran while one was open for 0% -> 1% of each run, Pallas kernels for 0% -> 0%
where the time goes in v4:
time: 68.5 us; the launch traced here: 68.2 us
  starting transfers between devices  29.8 us (44%)
  waiting for transfers between devices  26.7 us (39%)
  Pallas kernels  9.63 us (14%)
  local copies, waits for them, and re-layouts  0.92 us (1%)
    ppermute x17, waiting for transfers between devices, over_pcol(): return lax.ppermute(value, AXES, flat)  24.9 us
    ppermute x17, starting transfers between devices, over_pcol(): return lax.ppermute(value, AXES, flat)  19.6 us
    ppermute x4, starting transfers between devices, over_prow(): return lax.ppermute(value, AXES, flat)  10.2 us
    pallas_call x1, Pallas kernels, body(): pl.pallas_call(finish_kernel, out_shape=jax.ShapeDtypeStruct((rows, cols)...  9.34 us
    ppermute x4, waiting for transfers between devices, over_prow(): return lax.ppermute(value, AXES, flat)  1.79 us
  transfers between devices with their start and end apart: 21, of which 5 were waited for; matrix products, arithmetic and copies ran while one was open for 1% of the time, Pallas kernels for 0%

profile of v4, /device:TPU:1, one launch (start us, length us, event | category | flops | bytes accessed | tf_op | source)
XLA Modules:
  0.0 68.2 jit_solution(4452638195718591772)
XLA Ops:
  0.0 0.3 pack.1
  0.3 0.7 %collective-permute-start.5 = (f32[896,128]{1,0:T(8,128)}, f32[896,128]{1,0:T(8,128)S(1)}, u32[]{:S(2)}, u32[]{:S(2)}) collective-permute-start(f32[896,128]{1,0:T(8,128)} %get-tuple-element.23), channel_id=1, source_target_pairs={{0,5},{16,21},{32,37},{48,53},{64,69},{80,85},{96,101},{112,117},{... | collective-permute-start | bytes 1376264 | tf_op jit(solution)/shard_map/ppermute | solution.py:27
  1.0 0.7 %collective-permute-start.6 = (f32[896,128]{1,0:T(8,128)}, f32[896,128]{1,0:T(8,128)S(1)}, u32[]{:S(2)}, u32[]{:S(2)}) collective-permute-start(f32[896,128]{1,0:T(8,128)} %get-tuple-element.24), channel_id=1, source_target_pairs={{0,13},{16,29},{32,45},{48,61},{64,77},{80,93},{96,109},{112,125},... | collective-permute-start | bytes 1376264 | tf_op jit(solution)/shard_map/ppermute | solution.py:27
  1.7 0.7 %collective-permute-start = (f32[896,128]{1,0:T(8,128)}, f32[896,128]{1,0:T(8,128)S(1)}, u32[]{:S(2)}, u32[]{:S(2)}) collective-permute-start(f32[896,128]{1,0:T(8,128)} %get-tuple-element.18), channel_id=1, source_target_pairs={{0,4},{16,20},{32,36},{48,52},{64,68},{80,84},{96,100},{112,116},{... | collective-permute-start | bytes 1376264 | tf_op jit(solution)/shard_map/ppermute | solution.py:27
  2.4 0.7 %collective-permute-start.1 = (f32[896,128]{1,0:T(8,128)}, f32[896,128]{1,0:T(8,128)S(1)}, u32[]{:S(2)}, u32[]{:S(2)}) collective-permute-start(f32[896,128]{1,0:T(8,128)} %get-tuple-element.19), channel_id=1, source_target_pairs={{0,8},{16,24},{32,40},{48,56},{64,72},{80,88},{96,104},{112,120},{... | collective-permute-start | bytes 1376264 | tf_op jit(solution)/shard_map/ppermute | solution.py:27
  3.1 0.7 %collective-permute-start.2 = (f32[896,128]{1,0:T(8,128)}, f32[896,128]{1,0:T(8,128)S(1)}, u32[]{:S(2)}, u32[]{:S(2)}) collective-permute-start(f32[896,128]{1,0:T(8,128)} %get-tuple-element.20), channel_id=1, source_target_pairs={{0,10},{16,26},{32,42},{48,58},{64,74},{80,90},{96,106},{112,122},... | collective-permute-start | bytes 1376264 | tf_op jit(solution)/shard_map/ppermute | solution.py:27
  3.8 0.0 collective-permute-done.5
  3.8 0.7 %collective-permute-start.3 = (f32[896,128]{1,0:T(8,128)}, f32[896,128]{1,0:T(8,128)S(1)}, u32[]{:S(2)}, u32[]{:S(2)}) collective-permute-start(f32[896,128]{1,0:T(8,128)} %get-tuple-element.21), channel_id=1, source_target_pairs={{0,2},{16,18},{32,34},{48,50},{64,66},{80,82},{96,98},{112,114},{1... | collective-permute-start | bytes 1376264 | tf_op jit(solution)/shard_map/ppermute | solution.py:27
  4.5 0.0 collective-permute-done.6
  4.5 0.7 %collective-permute-start.4 = (f32[896,128]{1,0:T(8,128)}, f32[896,128]{1,0:T(8,128)S(1)}, u32[]{:S(2)}, u32[]{:S(2)}) collective-permute-start(f32[896,128]{1,0:T(8,128)} %get-tuple-element.22), channel_id=1, source_target_pairs={{0,12},{16,28},{32,44},{48,60},{64,76},{80,92},{96,108},{112,124},... | collective-permute-start | bytes 1376264 | tf_op jit(solution)/shard_map/ppermute | solution.py:27
  5.2 0.1 add.116
  5.3 0.0 collective-permute-done
  5.3 0.7 %collective-permute-start.7 = (f32[896,128]{1,0:T(8,128)S(1)}, f32[896,128]{1,0:T(8,128)S(1)}, u32[]{:S(2)}, u32[]{:S(2)}) collective-permute-start(f32[896,128]{1,0:T(8,128)S(1)} %add.116), channel_id=1, source_target_pairs={{5,6},{13,14},{21,22},{29,30},{37,38},{45,46},{53,54},{61,62},{69,... | collective-permute-start | bytes 1376264 | tf_op jit(solution)/shard_map/ppermute | solution.py:27
  6.0 0.0 collective-permute-done.1
  6.0 0.0 collective-permute-done.2
  6.0 0.0 collective-permute-done.3
  6.0 0.0 collective-permute-done.4
  6.0 0.0 collective-permute-done.7
  6.0 0.2 add_add_fusion
  6.2 1.3 %collective-permute-start.8 = (f32[896,128]{1,0:T(8,128)S(1)}, f32[896,128]{1,0:T(8,128)S(1)}, u32[]{:S(2)}, u32[]{:S(2)}) collective-permute-start(f32[896,128]{1,0:T(8,128)S(1)} %add_add_fusion), channel_id=1, source_target_pairs={{0,1},{2,3},{4,5},{6,7},{8,9},{10,11},{12,13},{14,15},{16,17},{18,... | collective-permute-start | bytes 1376264 | tf_op jit(solution)/shard_map/ppermute | solution.py:27
  7.6 20.7 %collective-permute-done.8 = f32[896,128]{1,0:T(8,128)S(1)} collective-permute-done((f32[896,128]{1,0:T(8,128)S(1)}, f32[896,128]{1,0:T(8,128)S(1)}, u32[]{:S(2)}, u32[]{:S(2)}) %collective-permute-start.8) | collective-permute-done | bytes 458784 | tf_op jit(solution)/shard_map/ppermute | solution.py:27
  28.4 4.4 %collective-permute-start.9 = (f32[2,64,128]{2,1,0:T(8,128)S(1)}, f32[2,64,128]{2,1,0:T(8,128)S(1)}, u32[]{:S(2)}, u32[]{:S(2)}) collective-permute-start(f32[2,64,128]{2,1,0:T(8,128)S(1)} %bitcast.44), channel_id=1, source_target_pairs={{0,48},{16,32},{32,16},{48,0},{64,112},{80,96},{96,80},{112,64},{1... | collective-permute-start | bytes 196616 | tf_op jit(solution)/shard_map/ppermute | solution.py:32
  32.8 2.5 %collective-permute-start.13 = (f32[768,128]{1,0:T(8,128)S(1)}, f32[768,128]{1,0:T(8,128)S(1)}, u32[]{:S(2)}, u32[]{:S(2)}) collective-permute-start(f32[768,128]{1,0:T(8,128)S(1)} %slice.59.refs_0_), channel_id=1, source_target_pairs={{0,6},{2,4},{4,10},{6,8},{8,14},{10,12},{12,2},{14,0},{1,15},{3,13... | collective-permute-start | bytes 1179656 | tf_op jit(solution)/shard_map/ppermute | solution.py:27
  35.3 0.0 collective-permute-start.12
  35.3 0.0 collective-permute-done.9
  35.4 1.4 %collective-permute-start.10 = (f32[3,64,128]{2,1,0:T(8,128)S(1)}, f32[3,64,128]{2,1,0:T(8,128)S(1)}, u32[]{:S(2)}, u32[]{:S(2)}) collective-permute-start(f32[3,64,128]{2,1,0:T(8,128)S(1)} %pad_maximum_fusion.1), channel_id=1, source_target_pairs={{0,64},{16,80},{32,96},{48,112},{64,0},{80,16},{96,32},{112,48},{1... | collective-permute-start | bytes 294920 | tf_op jit(solution)/shard_map/ppermute | solution.py:32
  36.8 0.7 collective-permute-start.14
  37.4 1.8 %collective-permute-done.10 = f32[3,64,128]{2,1,0:T(8,128)S(1)} collective-permute-done((f32[3,64,128]{2,1,0:T(8,128)S(1)}, f32[3,64,128]{2,1,0:T(8,128)S(1)}, u32[]{:S(2)}, u32[]{:S(2)}) %collective-permute-start.10) | collective-permute-done | bytes 98336 | tf_op jit(solution)/shard_map/ppermute | solution.py:32
  39.2 0.1 broadcast_select_fusion.1
  39.3 2.8 %collective-permute-start.11 = (f32[3,64,128]{2,1,0:T(8,128)S(1)}, f32[3,64,128]{2,1,0:T(8,128)S(1)}, u32[]{:S(2)}, u32[]{:S(2)}) collective-permute-start(f32[3,64,128]{2,1,0:T(8,128)S(1)} %broadcast_select_fusion.1), channel_id=1, source_target_pairs={{0,192},{16,208},{32,224},{48,240},{64,128},{80,144},{96,160},{112... | collective-permute-start | bytes 294920 | tf_op jit(solution)/shard_map/ppermute | solution.py:32
  42.1 2.2 %collective-permute-done.13.refs_5_ = f32[768,128]{1,0:T(8,128)S(1)} collective-permute-done((f32[768,128]{1,0:T(8,128)S(1)}, f32[768,128]{1,0:T(8,128)S(1)}, u32[]{:S(2)}, u32[]{:S(2)}) %collective-permute-start.13) | collective-permute-done | bytes 393248 | tf_op jit(solution)/shard_map/ppermute | solution.py:27
  44.2 0.0 copy-start
  44.3 0.7 %collective-permute-done.12.refs_3_ = f32[768,128]{1,0:T(8,128)S(1)} collective-permute-done((f32[768,128]{1,0:T(8,128)S(1)}, f32[768,128]{1,0:T(8,128)S(1)}, u32[]{:S(2)}, u32[]{:S(2)}) %collective-permute-start.12) | collective-permute-done | bytes 393248 | tf_op jit(solution)/shard_map/ppermute | solution.py:27
  45.0 0.1 broadcast_select_fusion
  45.0 2.3 %collective-permute-start.19 = (f32[768,128]{1,0:T(8,128)S(1)}, f32[768,128]{1,0:T(8,128)S(1)}, u32[]{:S(2)}, u32[]{:S(2)}) collective-permute-start(f32[768,128]{1,0:T(8,128)S(1)} %broadcast_select_fusion), channel_id=1, source_target_pairs={{0,4},{2,6},{4,8},{6,10},{8,12},{10,14},{12,0},{14,2},{1,13},{3,15... | collective-permute-start | bytes 1179656 | tf_op jit(solution)/shard_map/ppermute | solution.py:27
  47.4 0.0 collective-permute-done.11
  47.4 0.1 broadcast_select_fusion.2
  47.4 0.0 collective-permute-done.14.refs_1_
  47.5 1.7 %collective-permute-start.15 = (f32[3,64,128]{2,1,0:T(8,128)S(1)}, f32[3,64,128]{2,1,0:T(8,128)S(1)}, u32[]{:S(2)}, u32[]{:S(2)}) collective-permute-start(f32[3,64,128]{2,1,0:T(8,128)S(1)} %broadcast_select_fusion.2), channel_id=1, source_target_pairs={{0,16},{16,0},{32,48},{48,32},{64,80},{80,64},{96,112},{112,96},{1... | collective-permute-start | bytes 294920 | tf_op jit(solution)/shard_map/ppermute | solution.py:32
  49.1 0.1 stack.57.info
  49.2 1.3 %collective-permute-start.16 = (f32[768,128]{1,0:T(8,128)S(1)}, f32[768,128]{1,0:T(8,128)S(1)}, u32[]{:S(2)}, u32[]{:S(2)}) collective-permute-start(f32[768,128]{1,0:T(8,128)S(1)} %collective-permute-done.14.refs_1_), channel_id=1, source_target_pairs={{0,1},{2,3},{4,5},{6,7},{8,9},{10,11},{12,13},{14,15},{16,17},{18,... | collective-permute-start | bytes 1179656 | tf_op jit(solution)/shard_map/ppermute | solution.py:27
  50.5 1.7 %collective-permute-start.17 = (f32[768,128]{1,0:T(8,128)S(1)}, f32[768,128]{1,0:T(8,128)S(1)}, u32[]{:S(2)}, u32[]{:S(2)}) collective-permute-start(f32[768,128]{1,0:T(8,128)S(1)} %collective-permute-done.12.refs_3_), channel_id=1, source_target_pairs={{0,1},{1,0},{2,3},{3,2},{4,5},{5,4},{6,7},{7,6},{8,9},{9,8},{10,11... | collective-permute-start | bytes 1179656 | tf_op jit(solution)/shard_map/ppermute | solution.py:27
  52.3 0.1 collective-permute-start.18
  52.4 0.0 collective-permute-done.15
  52.4 0.0 collective-permute-done.19.refs_7_
  52.4 0.0 copy-start.1
  52.4 4.1 %collective-permute-start.20 = (f32[768,128]{1,0:T(8,128)S(1)}, f32[768,128]{1,0:T(8,128)S(1)}, u32[]{:S(2)}, u32[]{:S(2)}) collective-permute-start(f32[768,128]{1,0:T(8,128)S(1)} %collective-permute-done.19.refs_7_), channel_id=1, source_target_pairs={{0,1},{1,0},{2,3},{3,2},{4,5},{5,4},{6,7},{7,6},{8,9},{9,8},{10,11... | collective-permute-start | bytes 1179656 | tf_op jit(solution)/shard_map/ppermute | solution.py:27
  56.6 0.0 collective-permute-done.16.refs_2_
  56.6 0.0 collective-permute-done.17.refs_4_
  56.6 0.0 copy-start.2
  56.6 0.0 collective-permute-done.18.refs_6_
  56.6 0.0 copy-start.3
  56.6 1.2 %collective-permute-done.20.refs_8_ = f32[768,128]{1,0:T(8,128)S(1)} collective-permute-done((f32[768,128]{1,0:T(8,128)S(1)}, f32[768,128]{1,0:T(8,128)S(1)}, u32[]{:S(2)}, u32[]{:S(2)}) %collective-permute-start.20) | collective-permute-done | bytes 393248 | tf_op jit(solution)/shard_map/ppermute | solution.py:27
  57.9 0.0 copy-done
  57.9 0.0 copy-done.1
  57.9 0.0 copy-done.2
  57.9 0.0 copy-done.3
  57.9 0.0 copy-start.4
  57.9 0.8 %copy-done.4 = f32[768,128]{1,0:T(8,128)} copy-done((f32[768,128]{1,0:T(8,128)}, f32[768,128]{1,0:T(8,128)S(1)}, u32[]{:S(2)}) %copy-start.4) | copy-done | bytes 393240
  58.7 9.3 %finish.1 = f32[6144,256]{1,0:T(8,128)} custom-call(s32[11]{0:T(128)S(1)} %stack.57.info, f32[128,128]{1,0:T(8,128)S(1)} %pad_maximum_fusion.2.corner_ref, f32[256,128]{1,0:T(8,128)S(1)} %pad_maximum_fusion.lead_ref, f32[768,128]{1,0:T(8,128)S(1)} %slice.59.refs_0_, f32[768,128]{1,0:T(8,128)S(1)} %collective-permute-done.14.refs_1_, ...), custom_call_target="tpu_custom_call" | custom-call | tf_op jit(solution)/shard_map/finish/pallas_call | solution.py:282
  (12 shorter events, 0.2 us)
Async XLA Ops:
  0.3 3.5 %collective-permute-start.5 = (f32[896,128]{1,0:T(8,128)}, f32[896,128]{1,0:T(8,128)S(1)}, u32[]{:S(2)}, u32[]{:S(2)}) collective-permute-start(f32[896,128]{1,0:T(8,128)} %get-tuple-element.23), channel_id=1, source_target_pairs={{0,5},{16,21},{32,37},{48,53},{64,69},{80,85},{96,101},{112,117},{... | collective-permute-start | bytes 1376264 | tf_op jit(solution)/shard_map/ppermute | solution.py:27
  1.0 3.5 %collective-permute-start.6 = (f32[896,128]{1,0:T(8,128)}, f32[896,128]{1,0:T(8,128)S(1)}, u32[]{:S(2)}, u32[]{:S(2)}) collective-permute-start(f32[896,128]{1,0:T(8,128)} %get-tuple-element.24), channel_id=1, source_target_pairs={{0,13},{16,29},{32,45},{48,61},{64,77},{80,93},{96,109},{112,125},... | collective-permute-start | bytes 1376264 | tf_op jit(solution)/shard_map/ppermute | solution.py:27
  1.7 3.6 %collective-permute-start = (f32[896,128]{1,0:T(8,128)}, f32[896,128]{1,0:T(8,128)S(1)}, u32[]{:S(2)}, u32[]{:S(2)}) collective-permute-start(f32[896,128]{1,0:T(8,128)} %get-tuple-element.18), channel_id=1, source_target_pairs={{0,4},{16,20},{32,36},{48,52},{64,68},{80,84},{96,100},{112,116},{... | collective-permute-start | bytes 1376264 | tf_op jit(solution)/shard_map/ppermute | solution.py:27
  2.4 3.6 %collective-permute-start.1 = (f32[896,128]{1,0:T(8,128)}, f32[896,128]{1,0:T(8,128)S(1)}, u32[]{:S(2)}, u32[]{:S(2)}) collective-permute-start(f32[896,128]{1,0:T(8,128)} %get-tuple-element.19), channel_id=1, source_target_pairs={{0,8},{16,24},{32,40},{48,56},{64,72},{80,88},{96,104},{112,120},{... | collective-permute-start | bytes 1376264 | tf_op jit(solution)/shard_map/ppermute | solution.py:27
  3.1 2.9 %collective-permute-start.2 = (f32[896,128]{1,0:T(8,128)}, f32[896,128]{1,0:T(8,128)S(1)}, u32[]{:S(2)}, u32[]{:S(2)}) collective-permute-start(f32[896,128]{1,0:T(8,128)} %get-tuple-element.20), channel_id=1, source_target_pairs={{0,10},{16,26},{32,42},{48,58},{64,74},{80,90},{96,106},{112,122},... | collective-permute-start | bytes 1376264 | tf_op jit(solution)/shard_map/ppermute | solution.py:27
  3.8 2.2 %collective-permute-start.3 = (f32[896,128]{1,0:T(8,128)}, f32[896,128]{1,0:T(8,128)S(1)}, u32[]{:S(2)}, u32[]{:S(2)}) collective-permute-start(f32[896,128]{1,0:T(8,128)} %get-tuple-element.21), channel_id=1, source_target_pairs={{0,2},{16,18},{32,34},{48,50},{64,66},{80,82},{96,98},{112,114},{1... | collective-permute-start | bytes 1376264 | tf_op jit(solution)/shard_map/ppermute | solution.py:27
  4.5 1.5 %collective-permute-start.4 = (f32[896,128]{1,0:T(8,128)}, f32[896,128]{1,0:T(8,128)S(1)}, u32[]{:S(2)}, u32[]{:S(2)}) collective-permute-start(f32[896,128]{1,0:T(8,128)} %get-tuple-element.22), channel_id=1, source_target_pairs={{0,12},{16,28},{32,44},{48,60},{64,76},{80,92},{96,108},{112,124},... | collective-permute-start | bytes 1376264 | tf_op jit(solution)/shard_map/ppermute | solution.py:27
  5.3 0.7 %collective-permute-start.7 = (f32[896,128]{1,0:T(8,128)S(1)}, f32[896,128]{1,0:T(8,128)S(1)}, u32[]{:S(2)}, u32[]{:S(2)}) collective-permute-start(f32[896,128]{1,0:T(8,128)S(1)} %add.116), channel_id=1, source_target_pairs={{5,6},{13,14},{21,22},{29,30},{37,38},{45,46},{53,54},{61,62},{69,... | collective-permute-start | bytes 1376264 | tf_op jit(solution)/shard_map/ppermute | solution.py:27
  6.2 22.1 %collective-permute-start.8 = (f32[896,128]{1,0:T(8,128)S(1)}, f32[896,128]{1,0:T(8,128)S(1)}, u32[]{:S(2)}, u32[]{:S(2)}) collective-permute-start(f32[896,128]{1,0:T(8,128)S(1)} %add_add_fusion), channel_id=1, source_target_pairs={{0,1},{2,3},{4,5},{6,7},{8,9},{10,11},{12,13},{14,15},{16,17},{18,... | collective-permute-start | bytes 1376264 | tf_op jit(solution)/shard_map/ppermute | solution.py:27
  28.4 7.0 %collective-permute-start.9 = (f32[2,64,128]{2,1,0:T(8,128)S(1)}, f32[2,64,128]{2,1,0:T(8,128)S(1)}, u32[]{:S(2)}, u32[]{:S(2)}) collective-permute-start(f32[2,64,128]{2,1,0:T(8,128)S(1)} %bitcast.44), channel_id=1, source_target_pairs={{0,48},{16,32},{32,16},{48,0},{64,112},{80,96},{96,80},{112,64},{1... | collective-permute-start | bytes 196616 | tf_op jit(solution)/shard_map/ppermute | solution.py:32
  32.8 11.5 %collective-permute-start.13 = (f32[768,128]{1,0:T(8,128)S(1)}, f32[768,128]{1,0:T(8,128)S(1)}, u32[]{:S(2)}, u32[]{:S(2)}) collective-permute-start(f32[768,128]{1,0:T(8,128)S(1)} %slice.59.refs_0_), channel_id=1, source_target_pairs={{0,6},{2,4},{4,10},{6,8},{8,14},{10,12},{12,2},{14,0},{1,15},{3,13... | collective-permute-start | bytes 1179656 | tf_op jit(solution)/shard_map/ppermute | solution.py:27
  35.3 9.7 %collective-permute-start.12 = (f32[768,128]{1,0:T(8,128)S(1)}, f32[768,128]{1,0:T(8,128)S(1)}, u32[]{:S(2)}, u32[]{:S(2)}) collective-permute-start(f32[768,128]{1,0:T(8,128)S(1)} %slice.59.refs_0_), channel_id=1, source_target_pairs={{0,4},{2,6},{4,8},{6,10},{8,12},{10,14},{12,0},{14,2},{1,13},{3,15... | collective-permute-start | bytes 1179656 | tf_op jit(solution)/shard_map/ppermute | solution.py:27
  35.4 3.8 %collective-permute-start.10 = (f32[3,64,128]{2,1,0:T(8,128)S(1)}, f32[3,64,128]{2,1,0:T(8,128)S(1)}, u32[]{:S(2)}, u32[]{:S(2)}) collective-permute-start(f32[3,64,128]{2,1,0:T(8,128)S(1)} %pad_maximum_fusion.1), channel_id=1, source_target_pairs={{0,64},{16,80},{32,96},{48,112},{64,0},{80,16},{96,32},{112,48},{1... | collective-permute-start | bytes 294920 | tf_op jit(solution)/shard_map/ppermute | solution.py:32
  36.8 10.7 %collective-permute-start.14 = (f32[768,128]{1,0:T(8,128)S(1)}, f32[768,128]{1,0:T(8,128)S(1)}, u32[]{:S(2)}, u32[]{:S(2)}) collective-permute-start(f32[768,128]{1,0:T(8,128)S(1)} %slice.59.refs_0_), channel_id=1, source_target_pairs={{0,2},{2,0},{4,6},{6,4},{8,10},{10,8},{12,14},{14,12},{16,18},{18,... | collective-permute-start | bytes 1179656 | tf_op jit(solution)/shard_map/ppermute | solution.py:27
  39.3 8.1 %collective-permute-start.11 = (f32[3,64,128]{2,1,0:T(8,128)S(1)}, f32[3,64,128]{2,1,0:T(8,128)S(1)}, u32[]{:S(2)}, u32[]{:S(2)}) collective-permute-start(f32[3,64,128]{2,1,0:T(8,128)S(1)} %broadcast_select_fusion.1), channel_id=1, source_target_pairs={{0,192},{16,208},{32,224},{48,240},{64,128},{80,144},{96,160},{112... | collective-permute-start | bytes 294920 | tf_op jit(solution)/shard_map/ppermute | solution.py:32
  44.2 13.6 %copy-start = (f32[768,128]{1,0:T(8,128)}, f32[768,128]{1,0:T(8,128)S(1)}, u32[]{:S(2)}) copy-start(f32[768,128]{1,0:T(8,128)S(1)} %collective-permute-done.13.refs_5_) | copy-start | bytes 1179652
  45.0 7.4 %collective-permute-start.19 = (f32[768,128]{1,0:T(8,128)S(1)}, f32[768,128]{1,0:T(8,128)S(1)}, u32[]{:S(2)}, u32[]{:S(2)}) collective-permute-start(f32[768,128]{1,0:T(8,128)S(1)} %broadcast_select_fusion), channel_id=1, source_target_pairs={{0,4},{2,6},{4,8},{6,10},{8,12},{10,14},{12,0},{14,2},{1,13},{3,15... | collective-permute-start | bytes 1179656 | tf_op jit(solution)/shard_map/ppermute | solution.py:27
  47.5 4.9 %collective-permute-start.15 = (f32[3,64,128]{2,1,0:T(8,128)S(1)}, f32[3,64,128]{2,1,0:T(8,128)S(1)}, u32[]{:S(2)}, u32[]{:S(2)}) collective-permute-start(f32[3,64,128]{2,1,0:T(8,128)S(1)} %broadcast_select_fusion.2), channel_id=1, source_target_pairs={{0,16},{16,0},{32,48},{48,32},{64,80},{80,64},{96,112},{112,96},{1... | collective-permute-start | bytes 294920 | tf_op jit(solution)/shard_map/ppermute | solution.py:32
  49.2 7.3 %collective-permute-start.16 = (f32[768,128]{1,0:T(8,128)S(1)}, f32[768,128]{1,0:T(8,128)S(1)}, u32[]{:S(2)}, u32[]{:S(2)}) collective-permute-start(f32[768,128]{1,0:T(8,128)S(1)} %collective-permute-done.14.refs_1_), channel_id=1, source_target_pairs={{0,1},{2,3},{4,5},{6,7},{8,9},{10,11},{12,13},{14,15},{16,17},{18,... | collective-permute-start | bytes 1179656 | tf_op jit(solution)/shard_map/ppermute | solution.py:27
  50.5 6.1 %collective-permute-start.17 = (f32[768,128]{1,0:T(8,128)S(1)}, f32[768,128]{1,0:T(8,128)S(1)}, u32[]{:S(2)}, u32[]{:S(2)}) collective-permute-start(f32[768,128]{1,0:T(8,128)S(1)} %collective-permute-done.12.refs_3_), channel_id=1, source_target_pairs={{0,1},{1,0},{2,3},{3,2},{4,5},{5,4},{6,7},{7,6},{8,9},{9,8},{10,11... | collective-permute-start | bytes 1179656 | tf_op jit(solution)/shard_map/ppermute | solution.py:27
  52.3 4.3 %collective-permute-start.18 = (f32[768,128]{1,0:T(8,128)S(1)}, f32[768,128]{1,0:T(8,128)S(1)}, u32[]{:S(2)}, u32[]{:S(2)}) collective-permute-start(f32[768,128]{1,0:T(8,128)S(1)} %collective-permute-done.13.refs_5_), channel_id=1, source_target_pairs={{0,1},{1,0},{2,3},{3,2},{4,5},{5,4},{6,7},{7,6},{8,9},{9,8},{10,11... | collective-permute-start | bytes 1179656 | tf_op jit(solution)/shard_map/ppermute | solution.py:27
  52.4 5.5 %copy-start.1 = (f32[768,128]{1,0:T(8,128)}, f32[768,128]{1,0:T(8,128)S(1)}, u32[]{:S(2)}) copy-start(f32[768,128]{1,0:T(8,128)S(1)} %collective-permute-done.19.refs_7_) | copy-start | bytes 1179652
  52.4 5.5 %collective-permute-start.20 = (f32[768,128]{1,0:T(8,128)S(1)}, f32[768,128]{1,0:T(8,128)S(1)}, u32[]{:S(2)}, u32[]{:S(2)}) collective-permute-start(f32[768,128]{1,0:T(8,128)S(1)} %collective-permute-done.19.refs_7_), channel_id=1, source_target_pairs={{0,1},{1,0},{2,3},{3,2},{4,5},{5,4},{6,7},{7,6},{8,9},{9,8},{10,11... | collective-permute-start | bytes 1179656 | tf_op jit(solution)/shard_map/ppermute | solution.py:27
  56.6 1.3 %copy-start.2 = (f32[768,128]{1,0:T(8,128)}, f32[768,128]{1,0:T(8,128)S(1)}, u32[]{:S(2)}) copy-start(f32[768,128]{1,0:T(8,128)S(1)} %collective-permute-done.17.refs_4_) | copy-start | bytes 1179652
  56.6 1.3 %copy-start.3 = (f32[768,128]{1,0:T(8,128)}, f32[768,128]{1,0:T(8,128)S(1)}, u32[]{:S(2)}) copy-start(f32[768,128]{1,0:T(8,128)S(1)} %collective-permute-done.18.refs_6_) | copy-start | bytes 1179652
  57.9 0.8 %copy-start.4 = (f32[768,128]{1,0:T(8,128)}, f32[768,128]{1,0:T(8,128)S(1)}, u32[]{:S(2)}) copy-start(f32[768,128]{1,0:T(8,128)S(1)} %collective-permute-done.20.refs_8_) | copy-start | bytes 1179652

commit v5 on v4

--- a/solution.py
+++ b/solution.py
@@ -208,7 +208,7 @@
     hbm = pl.BlockSpec(memory_space=pl.ANY)
 
     messages = {}
-    for chips in ((3, 7, 2, 4, 5, 1, 6, 0),):
+    for chips in ((3, 7, 5, 2, 4, 1, 6, 0),):
         got = pl.pallas_call(
             functools.partial(pack_kernel, chips),
             out_shape=[jax.ShapeDtypeStruct((part + W2, W2), F32)] * len(chips),
@@ -224,7 +224,7 @@
         messages.update(zip(chips, got))
     relay = over_pcol(messages[3], [(0, 5)]) + over_pcol(messages[7], [(0, 13)])
     mine = jnp.where(is_src, messages[0], 0.0)
-    for g in (2, 4, 5, 1, 6):
+    for g in (5, 2, 4, 1, 6):
         mine = mine + over_pcol(messages[g], [(0, 2 * g)])
     mine = mine + over_pcol(relay, [(5, 6), (13, 14)])
     lend = [(2 * g, 2 * g + 1) for g in range(PIECES)]

time: 68.5 us -> 68.4 us (level)
    ppermute x17, waiting for transfers between devices: 24.9 us -> 23.6 us  [over_pcol(): return lax.ppermute(value, AXES, flat)]
    ppermute x4, waiting for transfers between devices: 1.79 us -> 2.87 us  [over_prow(): return lax.ppermute(value, AXES, flat)]
  transfers between devices with their start and end apart: 21 -> 21, of which waited for: 5 -> 6; matrix products, arithmetic and copies ran while one was open for 1% -> 1% of each run, Pallas kernels for 0% -> 0%
where the time goes in v5:
time: 68.4 us; the launch traced here: 68 us
  starting transfers between devices  29.9 us (44%)
  waiting for transfers between devices  26.4 us (39%)
  Pallas kernels  9.63 us (14%)
  local copies, waits for them, and re-layouts  0.92 us (1%)
    ppermute x17, waiting for transfers between devices, over_pcol(): return lax.ppermute(value, AXES, flat)  23.6 us
    ppermute x17, starting transfers between devices, over_pcol(): return lax.ppermute(value, AXES, flat)  20.1 us
    ppermute x4, starting transfers between devices, over_prow(): return lax.ppermute(value, AXES, flat)  9.79 us
    pallas_call x1, Pallas kernels, body(): pl.pallas_call(finish_kernel, out_shape=jax.ShapeDtypeStruct((rows, cols)...  9.34 us
    ppermute x4, waiting for transfers between devices, over_prow(): return lax.ppermute(value, AXES, flat)  2.87 us
  transfers between devices with their start and end apart: 21, of which 6 were waited for; matrix products, arithmetic and copies ran while one was open for 1% of the time, Pallas kernels for 0%

profile of v5, /device:TPU:1, one launch (start us, length us, event | category | flops | bytes accessed | tf_op | source)
XLA Modules:
  0.0 68.0 jit_solution(1556968382600379356)
XLA Ops:
  0.0 0.3 pack.1
  0.3 0.7 %collective-permute-start.5 = (f32[896,128]{1,0:T(8,128)}, f32[896,128]{1,0:T(8,128)S(1)}, u32[]{:S(2)}, u32[]{:S(2)}) collective-permute-start(f32[896,128]{1,0:T(8,128)} %get-tuple-element.23), channel_id=1, source_target_pairs={{0,5},{16,21},{32,37},{48,53},{64,69},{80,85},{96,101},{112,117},{... | collective-permute-start | bytes 1376264 | tf_op jit(solution)/shard_map/ppermute | solution.py:27
  1.0 0.7 %collective-permute-start.6 = (f32[896,128]{1,0:T(8,128)}, f32[896,128]{1,0:T(8,128)S(1)}, u32[]{:S(2)}, u32[]{:S(2)}) collective-permute-start(f32[896,128]{1,0:T(8,128)} %get-tuple-element.24), channel_id=1, source_target_pairs={{0,13},{16,29},{32,45},{48,61},{64,77},{80,93},{96,109},{112,125},... | collective-permute-start | bytes 1376264 | tf_op jit(solution)/shard_map/ppermute | solution.py:27
  1.7 0.7 %collective-permute-start = (f32[896,128]{1,0:T(8,128)}, f32[896,128]{1,0:T(8,128)S(1)}, u32[]{:S(2)}, u32[]{:S(2)}) collective-permute-start(f32[896,128]{1,0:T(8,128)} %get-tuple-element.18), channel_id=1, source_target_pairs={{0,10},{16,26},{32,42},{48,58},{64,74},{80,90},{96,106},{112,122},... | collective-permute-start | bytes 1376264 | tf_op jit(solution)/shard_map/ppermute | solution.py:27
  2.4 0.7 %collective-permute-start.1 = (f32[896,128]{1,0:T(8,128)}, f32[896,128]{1,0:T(8,128)S(1)}, u32[]{:S(2)}, u32[]{:S(2)}) collective-permute-start(f32[896,128]{1,0:T(8,128)} %get-tuple-element.19), channel_id=1, source_target_pairs={{0,4},{16,20},{32,36},{48,52},{64,68},{80,84},{96,100},{112,116},{... | collective-permute-start | bytes 1376264 | tf_op jit(solution)/shard_map/ppermute | solution.py:27
  3.1 0.7 %collective-permute-start.2 = (f32[896,128]{1,0:T(8,128)}, f32[896,128]{1,0:T(8,128)S(1)}, u32[]{:S(2)}, u32[]{:S(2)}) collective-permute-start(f32[896,128]{1,0:T(8,128)} %get-tuple-element.20), channel_id=1, source_target_pairs={{0,8},{16,24},{32,40},{48,56},{64,72},{80,88},{96,104},{112,120},{... | collective-permute-start | bytes 1376264 | tf_op jit(solution)/shard_map/ppermute | solution.py:27
  3.8 0.0 collective-permute-done.5
  3.8 0.7 %collective-permute-start.3 = (f32[896,128]{1,0:T(8,128)}, f32[896,128]{1,0:T(8,128)S(1)}, u32[]{:S(2)}, u32[]{:S(2)}) collective-permute-start(f32[896,128]{1,0:T(8,128)} %get-tuple-element.21), channel_id=1, source_target_pairs={{0,2},{16,18},{32,34},{48,50},{64,66},{80,82},{96,98},{112,114},{1... | collective-permute-start | bytes 1376264 | tf_op jit(solution)/shard_map/ppermute | solution.py:27
  4.5 0.0 collective-permute-done.6
  4.5 0.7 %collective-permute-start.4 = (f32[896,128]{1,0:T(8,128)}, f32[896,128]{1,0:T(8,128)S(1)}, u32[]{:S(2)}, u32[]{:S(2)}) collective-permute-start(f32[896,128]{1,0:T(8,128)} %get-tuple-element.22), channel_id=1, source_target_pairs={{0,12},{16,28},{32,44},{48,60},{64,76},{80,92},{96,108},{112,124},... | collective-permute-start | bytes 1376264 | tf_op jit(solution)/shard_map/ppermute | solution.py:27
  5.2 0.1 add.116
  5.3 0.0 collective-permute-done
  5.3 0.7 %collective-permute-start.7 = (f32[896,128]{1,0:T(8,128)S(1)}, f32[896,128]{1,0:T(8,128)S(1)}, u32[]{:S(2)}, u32[]{:S(2)}) collective-permute-start(f32[896,128]{1,0:T(8,128)S(1)} %add.116), channel_id=1, source_target_pairs={{5,6},{13,14},{21,22},{29,30},{37,38},{45,46},{53,54},{61,62},{69,... | collective-permute-start | bytes 1376264 | tf_op jit(solution)/shard_map/ppermute | solution.py:27
  6.0 0.0 collective-permute-done.1
  6.0 0.0 collective-permute-done.2
  6.0 0.0 collective-permute-done.3
  6.0 0.0 collective-permute-done.4
  6.0 0.0 collective-permute-done.7
  6.0 0.2 add_add_fusion
  6.2 1.3 %collective-permute-start.8 = (f32[896,128]{1,0:T(8,128)S(1)}, f32[896,128]{1,0:T(8,128)S(1)}, u32[]{:S(2)}, u32[]{:S(2)}) collective-permute-start(f32[896,128]{1,0:T(8,128)S(1)} %add_add_fusion), channel_id=1, source_target_pairs={{0,1},{2,3},{4,5},{6,7},{8,9},{10,11},{12,13},{14,15},{16,17},{18,... | collective-permute-start | bytes 1376264 | tf_op jit(solution)/shard_map/ppermute | solution.py:27
  7.6 20.3 %collective-permute-done.8 = f32[896,128]{1,0:T(8,128)S(1)} collective-permute-done((f32[896,128]{1,0:T(8,128)S(1)}, f32[896,128]{1,0:T(8,128)S(1)}, u32[]{:S(2)}, u32[]{:S(2)}) %collective-permute-start.8) | collective-permute-done | bytes 458784 | tf_op jit(solution)/shard_map/ppermute | solution.py:27
  28.0 4.4 %collective-permute-start.9 = (f32[2,64,128]{2,1,0:T(8,128)S(1)}, f32[2,64,128]{2,1,0:T(8,128)S(1)}, u32[]{:S(2)}, u32[]{:S(2)}) collective-permute-start(f32[2,64,128]{2,1,0:T(8,128)S(1)} %bitcast.44), channel_id=1, source_target_pairs={{0,48},{16,32},{32,16},{48,0},{64,112},{80,96},{96,80},{112,64},{1... | collective-permute-start | bytes 196616 | tf_op jit(solution)/shard_map/ppermute | solution.py:32
  32.4 2.9 %collective-permute-start.13 = (f32[768,128]{1,0:T(8,128)S(1)}, f32[768,128]{1,0:T(8,128)S(1)}, u32[]{:S(2)}, u32[]{:S(2)}) collective-permute-start(f32[768,128]{1,0:T(8,128)S(1)} %slice.59.refs_0_), channel_id=1, source_target_pairs={{0,6},{2,4},{4,10},{6,8},{8,14},{10,12},{12,2},{14,0},{1,15},{3,13... | collective-permute-start | bytes 1179656 | tf_op jit(solution)/shard_map/ppermute | solution.py:27
  35.3 0.0 collective-permute-start.12
  35.3 0.0 collective-permute-done.9
  35.4 1.4 %collective-permute-start.10 = (f32[3,64,128]{2,1,0:T(8,128)S(1)}, f32[3,64,128]{2,1,0:T(8,128)S(1)}, u32[]{:S(2)}, u32[]{:S(2)}) collective-permute-start(f32[3,64,128]{2,1,0:T(8,128)S(1)} %pad_maximum_fusion.1), channel_id=1, source_target_pairs={{0,64},{16,80},{32,96},{48,112},{64,0},{80,16},{96,32},{112,48},{1... | collective-permute-start | bytes 294920 | tf_op jit(solution)/shard_map/ppermute | solution.py:32
  36.8 0.7 collective-permute-start.14
  37.4 2.4 %collective-permute-done.10 = f32[3,64,128]{2,1,0:T(8,128)S(1)} collective-permute-done((f32[3,64,128]{2,1,0:T(8,128)S(1)}, f32[3,64,128]{2,1,0:T(8,128)S(1)}, u32[]{:S(2)}, u32[]{:S(2)}) %collective-permute-start.10) | collective-permute-done | bytes 98336 | tf_op jit(solution)/shard_map/ppermute | solution.py:32
  39.8 0.1 broadcast_select_fusion.1
  39.9 2.8 %collective-permute-start.11 = (f32[3,64,128]{2,1,0:T(8,128)S(1)}, f32[3,64,128]{2,1,0:T(8,128)S(1)}, u32[]{:S(2)}, u32[]{:S(2)}) collective-permute-start(f32[3,64,128]{2,1,0:T(8,128)S(1)} %broadcast_select_fusion.1), channel_id=1, source_target_pairs={{0,192},{16,208},{32,224},{48,240},{64,128},{80,144},{96,160},{112... | collective-permute-start | bytes 294920 | tf_op jit(solution)/shard_map/ppermute | solution.py:32
  42.7 1.6 %collective-permute-done.13.refs_5_ = f32[768,128]{1,0:T(8,128)S(1)} collective-permute-done((f32[768,128]{1,0:T(8,128)S(1)}, f32[768,128]{1,0:T(8,128)S(1)}, u32[]{:S(2)}, u32[]{:S(2)}) %collective-permute-start.13) | collective-permute-done | bytes 393248 | tf_op jit(solution)/shard_map/ppermute | solution.py:27
  44.2 0.0 copy-start
  44.2 0.4 collective-permute-done.12.refs_3_
  44.6 0.1 broadcast_select_fusion
  44.7 2.7 %collective-permute-start.19 = (f32[768,128]{1,0:T(8,128)S(1)}, f32[768,128]{1,0:T(8,128)S(1)}, u32[]{:S(2)}, u32[]{:S(2)}) collective-permute-start(f32[768,128]{1,0:T(8,128)S(1)} %broadcast_select_fusion), channel_id=1, source_target_pairs={{0,4},{2,6},{4,8},{6,10},{8,12},{10,14},{12,0},{14,2},{1,13},{3,15... | collective-permute-start | bytes 1179656 | tf_op jit(solution)/shard_map/ppermute | solution.py:27
  47.4 0.0 collective-permute-done.11
  47.4 0.1 broadcast_select_fusion.2
  47.4 0.0 collective-permute-done.14.refs_1_
  47.5 1.3 %collective-permute-start.15 = (f32[3,64,128]{2,1,0:T(8,128)S(1)}, f32[3,64,128]{2,1,0:T(8,128)S(1)}, u32[]{:S(2)}, u32[]{:S(2)}) collective-permute-start(f32[3,64,128]{2,1,0:T(8,128)S(1)} %broadcast_select_fusion.2), channel_id=1, source_target_pairs={{0,16},{16,0},{32,48},{48,32},{64,80},{80,64},{96,112},{112,96},{1... | collective-permute-start | bytes 294920 | tf_op jit(solution)/shard_map/ppermute | solution.py:32
  48.7 0.1 stack.57.info
  48.8 1.3 %collective-permute-start.16 = (f32[768,128]{1,0:T(8,128)S(1)}, f32[768,128]{1,0:T(8,128)S(1)}, u32[]{:S(2)}, u32[]{:S(2)}) collective-permute-start(f32[768,128]{1,0:T(8,128)S(1)} %collective-permute-done.14.refs_1_), channel_id=1, source_target_pairs={{0,1},{2,3},{4,5},{6,7},{8,9},{10,11},{12,13},{14,15},{16,17},{18,... | collective-permute-start | bytes 1179656 | tf_op jit(solution)/shard_map/ppermute | solution.py:27
  50.1 1.5 %collective-permute-start.17 = (f32[768,128]{1,0:T(8,128)S(1)}, f32[768,128]{1,0:T(8,128)S(1)}, u32[]{:S(2)}, u32[]{:S(2)}) collective-permute-start(f32[768,128]{1,0:T(8,128)S(1)} %collective-permute-done.12.refs_3_), channel_id=1, source_target_pairs={{0,1},{1,0},{2,3},{3,2},{4,5},{5,4},{6,7},{7,6},{8,9},{9,8},{10,11... | collective-permute-start | bytes 1179656 | tf_op jit(solution)/shard_map/ppermute | solution.py:27
  51.6 0.1 collective-permute-start.18
  51.7 0.5 collective-permute-done.15
  52.2 0.0 collective-permute-done.19.refs_7_
  52.2 0.0 copy-start.1
  52.2 4.1 %collective-permute-start.20 = (f32[768,128]{1,0:T(8,128)S(1)}, f32[768,128]{1,0:T(8,128)S(1)}, u32[]{:S(2)}, u32[]{:S(2)}) collective-permute-start(f32[768,128]{1,0:T(8,128)S(1)} %collective-permute-done.19.refs_7_), channel_id=1, source_target_pairs={{0,1},{1,0},{2,3},{3,2},{4,5},{5,4},{6,7},{7,6},{8,9},{9,8},{10,11... | collective-permute-start | bytes 1179656 | tf_op jit(solution)/shard_map/ppermute | solution.py:27
  56.4 0.0 collective-permute-done.16.refs_2_
  56.4 0.0 collective-permute-done.17.refs_4_
  56.5 0.0 copy-start.2
  56.5 0.0 collective-permute-done.18.refs_6_
  56.5 0.0 copy-start.3
  56.5 1.2 %collective-permute-done.20.refs_8_ = f32[768,128]{1,0:T(8,128)S(1)} collective-permute-done((f32[768,128]{1,0:T(8,128)S(1)}, f32[768,128]{1,0:T(8,128)S(1)}, u32[]{:S(2)}, u32[]{:S(2)}) %collective-permute-start.20) | collective-permute-done | bytes 393248 | tf_op jit(solution)/shard_map/ppermute | solution.py:27
  57.7 0.0 copy-done
  57.7 0.0 copy-done.1
  57.7 0.0 copy-done.2
  57.7 0.0 copy-done.3
  57.8 0.0 copy-start.4
  57.8 0.8 %copy-done.4 = f32[768,128]{1,0:T(8,128)} copy-done((f32[768,128]{1,0:T(8,128)}, f32[768,128]{1,0:T(8,128)S(1)}, u32[]{:S(2)}) %copy-start.4) | copy-done | bytes 393240
  58.5 9.3 %finish.1 = f32[6144,256]{1,0:T(8,128)} custom-call(s32[11]{0:T(128)S(1)} %stack.57.info, f32[128,128]{1,0:T(8,128)S(1)} %pad_maximum_fusion.2.corner_ref, f32[256,128]{1,0:T(8,128)S(1)} %pad_maximum_fusion.lead_ref, f32[768,128]{1,0:T(8,128)S(1)} %slice.59.refs_0_, f32[768,128]{1,0:T(8,128)S(1)} %collective-permute-done.14.refs_1_, ...), custom_call_target="tpu_custom_call" | custom-call | tf_op jit(solution)/shard_map/finish/pallas_call | solution.py:282
  (12 shorter events, 0.2 us)
Async XLA Ops:
  0.3 3.5 %collective-permute-start.5 = (f32[896,128]{1,0:T(8,128)}, f32[896,128]{1,0:T(8,128)S(1)}, u32[]{:S(2)}, u32[]{:S(2)}) collective-permute-start(f32[896,128]{1,0:T(8,128)} %get-tuple-element.23), channel_id=1, source_target_pairs={{0,5},{16,21},{32,37},{48,53},{64,69},{80,85},{96,101},{112,117},{... | collective-permute-start | bytes 1376264 | tf_op jit(solution)/shard_map/ppermute | solution.py:27
  1.0 3.5 %collective-permute-start.6 = (f32[896,128]{1,0:T(8,128)}, f32[896,128]{1,0:T(8,128)S(1)}, u32[]{:S(2)}, u32[]{:S(2)}) collective-permute-start(f32[896,128]{1,0:T(8,128)} %get-tuple-element.24), channel_id=1, source_target_pairs={{0,13},{16,29},{32,45},{48,61},{64,77},{80,93},{96,109},{112,125},... | collective-permute-start | bytes 1376264 | tf_op jit(solution)/shard_map/ppermute | solution.py:27
  1.7 3.6 %collective-permute-start = (f32[896,128]{1,0:T(8,128)}, f32[896,128]{1,0:T(8,128)S(1)}, u32[]{:S(2)}, u32[]{:S(2)}) collective-permute-start(f32[896,128]{1,0:T(8,128)} %get-tuple-element.18), channel_id=1, source_target_pairs={{0,10},{16,26},{32,42},{48,58},{64,74},{80,90},{96,106},{112,122},... | collective-permute-start | bytes 1376264 | tf_op jit(solution)/shard_map/ppermute | solution.py:27
  2.4 3.6 %collective-permute-start.1 = (f32[896,128]{1,0:T(8,128)}, f32[896,128]{1,0:T(8,128)S(1)}, u32[]{:S(2)}, u32[]{:S(2)}) collective-permute-start(f32[896,128]{1,0:T(8,128)} %get-tuple-element.19), channel_id=1, source_target_pairs={{0,4},{16,20},{32,36},{48,52},{64,68},{80,84},{96,100},{112,116},{... | collective-permute-start | bytes 1376264 | tf_op jit(solution)/shard_map/ppermute | solution.py:27
  3.1 2.9 %collective-permute-start.2 = (f32[896,128]{1,0:T(8,128)}, f32[896,128]{1,0:T(8,128)S(1)}, u32[]{:S(2)}, u32[]{:S(2)}) collective-permute-start(f32[896,128]{1,0:T(8,128)} %get-tuple-element.20), channel_id=1, source_target_pairs={{0,8},{16,24},{32,40},{48,56},{64,72},{80,88},{96,104},{112,120},{... | collective-permute-start | bytes 1376264 | tf_op jit(solution)/shard_map/ppermute | solution.py:27
  3.8 2.2 %collective-permute-start.3 = (f32[896,128]{1,0:T(8,128)}, f32[896,128]{1,0:T(8,128)S(1)}, u32[]{:S(2)}, u32[]{:S(2)}) collective-permute-start(f32[896,128]{1,0:T(8,128)} %get-tuple-element.21), channel_id=1, source_target_pairs={{0,2},{16,18},{32,34},{48,50},{64,66},{80,82},{96,98},{112,114},{1... | collective-permute-start | bytes 1376264 | tf_op jit(solution)/shard_map/ppermute | solution.py:27
  4.5 1.5 %collective-permute-start.4 = (f32[896,128]{1,0:T(8,128)}, f32[896,128]{1,0:T(8,128)S(1)}, u32[]{:S(2)}, u32[]{:S(2)}) collective-permute-start(f32[896,128]{1,0:T(8,128)} %get-tuple-element.22), channel_id=1, source_target_pairs={{0,12},{16,28},{32,44},{48,60},{64,76},{80,92},{96,108},{112,124},... | collective-permute-start | bytes 1376264 | tf_op jit(solution)/shard_map/ppermute | solution.py:27
  5.3 0.7 %collective-permute-start.7 = (f32[896,128]{1,0:T(8,128)S(1)}, f32[896,128]{1,0:T(8,128)S(1)}, u32[]{:S(2)}, u32[]{:S(2)}) collective-permute-start(f32[896,128]{1,0:T(8,128)S(1)} %add.116), channel_id=1, source_target_pairs={{5,6},{13,14},{21,22},{29,30},{37,38},{45,46},{53,54},{61,62},{69,... | collective-permute-start | bytes 1376264 | tf_op jit(solution)/shard_map/ppermute | solution.py:27
  6.2 21.7 %collective-permute-start.8 = (f32[896,128]{1,0:T(8,128)S(1)}, f32[896,128]{1,0:T(8,128)S(1)}, u32[]{:S(2)}, u32[]{:S(2)}) collective-permute-start(f32[896,128]{1,0:T(8,128)S(1)} %add_add_fusion), channel_id=1, source_target_pairs={{0,1},{2,3},{4,5},{6,7},{8,9},{10,11},{12,13},{14,15},{16,17},{18,... | collective-permute-start | bytes 1376264 | tf_op jit(solution)/shard_map/ppermute | solution.py:27
  28.0 7.3 %collective-permute-start.9 = (f32[2,64,128]{2,1,0:T(8,128)S(1)}, f32[2,64,128]{2,1,0:T(8,128)S(1)}, u32[]{:S(2)}, u32[]{:S(2)}) collective-permute-start(f32[2,64,128]{2,1,0:T(8,128)S(1)} %bitcast.44), channel_id=1, source_target_pairs={{0,48},{16,32},{32,16},{48,0},{64,112},{80,96},{96,80},{112,64},{1... | collective-permute-start | bytes 196616 | tf_op jit(solution)/shard_map/ppermute | solution.py:32
  32.4 11.8 %collective-permute-start.13 = (f32[768,128]{1,0:T(8,128)S(1)}, f32[768,128]{1,0:T(8,128)S(1)}, u32[]{:S(2)}, u32[]{:S(2)}) collective-permute-start(f32[768,128]{1,0:T(8,128)S(1)} %slice.59.refs_0_), channel_id=1, source_target_pairs={{0,6},{2,4},{4,10},{6,8},{8,14},{10,12},{12,2},{14,0},{1,15},{3,13... | collective-permute-start | bytes 1179656 | tf_op jit(solution)/shard_map/ppermute | solution.py:27
  35.3 9.3 %collective-permute-start.12 = (f32[768,128]{1,0:T(8,128)S(1)}, f32[768,128]{1,0:T(8,128)S(1)}, u32[]{:S(2)}, u32[]{:S(2)}) collective-permute-start(f32[768,128]{1,0:T(8,128)S(1)} %slice.59.refs_0_), channel_id=1, source_target_pairs={{0,4},{2,6},{4,8},{6,10},{8,12},{10,14},{12,0},{14,2},{1,13},{3,15... | collective-permute-start | bytes 1179656 | tf_op jit(solution)/shard_map/ppermute | solution.py:27
  35.4 4.4 %collective-permute-start.10 = (f32[3,64,128]{2,1,0:T(8,128)S(1)}, f32[3,64,128]{2,1,0:T(8,128)S(1)}, u32[]{:S(2)}, u32[]{:S(2)}) collective-permute-start(f32[3,64,128]{2,1,0:T(8,128)S(1)} %pad_maximum_fusion.1), channel_id=1, source_target_pairs={{0,64},{16,80},{32,96},{48,112},{64,0},{80,16},{96,32},{112,48},{1... | collective-permute-start | bytes 294920 | tf_op jit(solution)/shard_map/ppermute | solution.py:32
  36.8 10.7 %collective-permute-start.14 = (f32[768,128]{1,0:T(8,128)S(1)}, f32[768,128]{1,0:T(8,128)S(1)}, u32[]{:S(2)}, u32[]{:S(2)}) collective-permute-start(f32[768,128]{1,0:T(8,128)S(1)} %slice.59.refs_0_), channel_id=1, source_target_pairs={{0,2},{2,0},{4,6},{6,4},{8,10},{10,8},{12,14},{14,12},{16,18},{18,... | collective-permute-start | bytes 1179656 | tf_op jit(solution)/shard_map/ppermute | solution.py:27
  39.9 7.5 %collective-permute-start.11 = (f32[3,64,128]{2,1,0:T(8,128)S(1)}, f32[3,64,128]{2,1,0:T(8,128)S(1)}, u32[]{:S(2)}, u32[]{:S(2)}) collective-permute-start(f32[3,64,128]{2,1,0:T(8,128)S(1)} %broadcast_select_fusion.1), channel_id=1, source_target_pairs={{0,192},{16,208},{32,224},{48,240},{64,128},{80,144},{96,160},{112... | collective-permute-start | bytes 294920 | tf_op jit(solution)/shard_map/ppermute | solution.py:32
  44.2 13.5 %copy-start = (f32[768,128]{1,0:T(8,128)}, f32[768,128]{1,0:T(8,128)S(1)}, u32[]{:S(2)}) copy-start(f32[768,128]{1,0:T(8,128)S(1)} %collective-permute-done.13.refs_5_) | copy-start | bytes 1179652
  44.7 7.6 %collective-permute-start.19 = (f32[768,128]{1,0:T(8,128)S(1)}, f32[768,128]{1,0:T(8,128)S(1)}, u32[]{:S(2)}, u32[]{:S(2)}) collective-permute-start(f32[768,128]{1,0:T(8,128)S(1)} %broadcast_select_fusion), channel_id=1, source_target_pairs={{0,4},{2,6},{4,8},{6,10},{8,12},{10,14},{12,0},{14,2},{1,13},{3,15... | collective-permute-start | bytes 1179656 | tf_op jit(solution)/shard_map/ppermute | solution.py:27
  47.5 4.7 %collective-permute-start.15 = (f32[3,64,128]{2,1,0:T(8,128)S(1)}, f32[3,64,128]{2,1,0:T(8,128)S(1)}, u32[]{:S(2)}, u32[]{:S(2)}) collective-permute-start(f32[3,64,128]{2,1,0:T(8,128)S(1)} %broadcast_select_fusion.2), channel_id=1, source_target_pairs={{0,16},{16,0},{32,48},{48,32},{64,80},{80,64},{96,112},{112,96},{1... | collective-permute-start | bytes 294920 | tf_op jit(solution)/shard_map/ppermute | solution.py:32
  48.8 7.6 %collective-permute-start.16 = (f32[768,128]{1,0:T(8,128)S(1)}, f32[768,128]{1,0:T(8,128)S(1)}, u32[]{:S(2)}, u32[]{:S(2)}) collective-permute-start(f32[768,128]{1,0:T(8,128)S(1)} %collective-permute-done.14.refs_1_), channel_id=1, source_target_pairs={{0,1},{2,3},{4,5},{6,7},{8,9},{10,11},{12,13},{14,15},{16,17},{18,... | collective-permute-start | bytes 1179656 | tf_op jit(solution)/shard_map/ppermute | solution.py:27
  50.1 6.4 %collective-permute-start.17 = (f32[768,128]{1,0:T(8,128)S(1)}, f32[768,128]{1,0:T(8,128)S(1)}, u32[]{:S(2)}, u32[]{:S(2)}) collective-permute-start(f32[768,128]{1,0:T(8,128)S(1)} %collective-permute-done.12.refs_3_), channel_id=1, source_target_pairs={{0,1},{1,0},{2,3},{3,2},{4,5},{5,4},{6,7},{7,6},{8,9},{9,8},{10,11... | collective-permute-start | bytes 1179656 | tf_op jit(solution)/shard_map/ppermute | solution.py:27
  51.6 4.9 %collective-permute-start.18 = (f32[768,128]{1,0:T(8,128)S(1)}, f32[768,128]{1,0:T(8,128)S(1)}, u32[]{:S(2)}, u32[]{:S(2)}) collective-permute-start(f32[768,128]{1,0:T(8,128)S(1)} %collective-permute-done.13.refs_5_), channel_id=1, source_target_pairs={{0,1},{1,0},{2,3},{3,2},{4,5},{5,4},{6,7},{7,6},{8,9},{9,8},{10,11... | collective-permute-start | bytes 1179656 | tf_op jit(solution)/shard_map/ppermute | solution.py:27
  52.2 5.5 %copy-start.1 = (f32[768,128]{1,0:T(8,128)}, f32[768,128]{1,0:T(8,128)S(1)}, u32[]{:S(2)}) copy-start(f32[768,128]{1,0:T(8,128)S(1)} %collective-permute-done.19.refs_7_) | copy-start | bytes 1179652
  52.2 5.5 %collective-permute-start.20 = (f32[768,128]{1,0:T(8,128)S(1)}, f32[768,128]{1,0:T(8,128)S(1)}, u32[]{:S(2)}, u32[]{:S(2)}) collective-permute-start(f32[768,128]{1,0:T(8,128)S(1)} %collective-permute-done.19.refs_7_), channel_id=1, source_target_pairs={{0,1},{1,0},{2,3},{3,2},{4,5},{5,4},{6,7},{7,6},{8,9},{9,8},{10,11... | collective-permute-start | bytes 1179656 | tf_op jit(solution)/shard_map/ppermute | solution.py:27
  56.5 1.3 %copy-start.2 = (f32[768,128]{1,0:T(8,128)}, f32[768,128]{1,0:T(8,128)S(1)}, u32[]{:S(2)}) copy-start(f32[768,128]{1,0:T(8,128)S(1)} %collective-permute-done.17.refs_4_) | copy-start | bytes 1179652
  56.5 1.3 %copy-start.3 = (f32[768,128]{1,0:T(8,128)}, f32[768,128]{1,0:T(8,128)S(1)}, u32[]{:S(2)}) copy-start(f32[768,128]{1,0:T(8,128)S(1)} %collective-permute-done.18.refs_6_) | copy-start | bytes 1179652
  57.8 0.8 %copy-start.4 = (f32[768,128]{1,0:T(8,128)}, f32[768,128]{1,0:T(8,128)S(1)}, u32[]{:S(2)}) copy-start(f32[768,128]{1,0:T(8,128)S(1)} %collective-permute-done.20.refs_8_) | copy-start | bytes 1179652
